TPU v7x, 256 devices: a whole 4x4x8 slice. The times are simulated.
256 devices in a mesh: shard: 64 (over y, z_lo, x, core), rep: 4 (over z_hi).
Axes of the slice: x: 4, y: 4, z: 8 (z_hi: 4, z_lo: 2; z = z_hi * 2 + z_lo), core: 2. Of those that a mesh axis runs over, the one named last changes fastest.
Arguments:
- pooled_grad: float32 [1024, 4, 64, 256], P('shard', 'rep'), may hold values from -0.8 to 0.8
- bag_lengths: int32 [64, 4, 1024], P('shard', 'rep'), may hold values from 1 to 64, 16384 in all within a row
- row_slots: int32 [64, 4, 16384], P('shard', 'rep'), may hold values from 0 to 511
- id_weights: int32 [64, 4, 16384], P('shard', 'rep'), may hold values from 1 to 32
- touched_rows: float32 [64, 512, 256], P('shard'), may hold values from -6 to 6
- accumulator: float32 [64, 512], P('shard'), may hold values from 0.005 to 0.5
Outputs:
- row_grad: float32 [64, 512, 256], P('shard', 'rep')
- updated_rows: float32 [64, 512, 256], P('shard')
Inputs may be any that keep to these rules, and one draw needn't show every extreme that they name: `bag_lengths`: in each table and replica group the bag lengths sum to 16384.
All inputs are finite; a program needn't handle non-finite values.
Results may differ from a plain program's by a relative error of at most 0.0003.
Values sent between devices are 32-bit elements; how exact they have to be, the bound alone decides.
No kernel may reach another device: no remote copies, remote signals or barrier semaphores. Data moves between devices by JAX's collectives and lax.ppermute only.
A program may use at most 64 MiB of HBM per device.

v0:
```python
import jax
import jax.numpy as jnp
from jax import lax
from jax.sharding import PartitionSpec as P

learn_rate = 0.5


def cut_along(array, dim, count):
    shape = array.shape
    pieces = array.reshape(*shape[:dim], count, shape[dim] // count, *shape[dim + 1 :])
    return jnp.moveaxis(pieces, dim, 0)


def summed_on_arrival(array, axis, dim):
    pieces = cut_along(array, dim, lax.axis_size(axis))
    arrived = lax.all_to_all(pieces, axis, split_axis=0, concat_axis=0, tiled=True)
    return arrived.sum(axis=0)


def copy_for_each(array, axis):
    count = lax.axis_size(axis)
    return lax.all_to_all(
        jnp.broadcast_to(array[None], (count, *array.shape)), axis, 0, 0, tiled=True
    )


def in_order(pieces, dim):
    shape = list(pieces.shape[1:])
    shape[dim] *= pieces.shape[0]
    return jnp.moveaxis(pieces, 0, dim).reshape(shape)


def collect(array, axis, dim):
    pieces = copy_for_each(array, axis)
    return in_order(pieces, dim)


def table_rows(arrived, lengths, slots, weights, height):
    ends = jnp.cumsum(lengths)
    starts = ends - lengths
    count = slots.shape[0]
    span = min(512, count)
    turns = count // span
    slot_ids = jnp.arange(height, dtype=jnp.int32)

    def add_block(step, total):
        start = step * span
        positions = start + jnp.arange(span, dtype=jnp.int32)
        target = lax.dynamic_slice_in_dim(slots, start, span)
        factor = lax.dynamic_slice_in_dim(weights, start, span)
        chosen = jnp.where(target[:, None] == slot_ids[None, :], factor[:, None], 0).astype(
            jnp.bfloat16
        )
        member = (
            (positions[:, None] >= starts[None, :]) & (positions[:, None] < ends[None, :])
        ).astype(jnp.bfloat16)
        return total + lax.dot_general(
            chosen, member, (((0,), (0,)), ((), ())), preferred_element_type=jnp.float32
        )

    empty = jnp.zeros((height, arrived.shape[0]), jnp.float32)
    tallies = lax.fori_loop(0, turns, add_block, empty)
    return (
        jnp.dot(
            tallies, arrived, precision=lax.Precision.HIGHEST, preferred_element_type=jnp.float32
        )
        * 0.0625
    )


def adagrad(rows, state, grads):
    new_state = state + jnp.mean(grads * grads, axis=-1)
    return rows - learn_rate * grads / (jnp.sqrt(new_state)[..., None] + 1e-08)


def per_device(pooled_grad, bag_lengths, row_slots, id_weights, touched_rows, accumulator):
    arrived = lax.all_to_all(pooled_grad, "shard", split_axis=2, concat_axis=0, tiled=True)
    height = touched_rows.shape[1]
    owned = touched_rows.shape[0]
    local = jnp.stack(
        [table_rows(arrived[:, 0, 0], bag_lengths[0, 0], row_slots[0, 0], id_weights[0, 0], height)]
    )
    count = height // lax.axis_size("rep")
    start = lax.axis_index("rep") * count
    grad_part = summed_on_arrival(local, "rep", 1)
    rows_part = lax.dynamic_slice_in_dim(touched_rows, start, count, 1)
    state_part = lax.dynamic_slice_in_dim(accumulator, start, count, 1)
    fresh = adagrad(rows_part, state_part, grad_part)
    updated = collect(fresh, "rep", 1)
    return (grad_part, updated)


def solution(mesh):
    placed = (
        P("shard", "rep", None, None),
        P("shard", "rep", None),
        P("shard", "rep", None),
        P("shard", "rep", None),
        P("shard", None, None),
        P("shard", None),
    )
    return jax.shard_map(
        per_device,
        mesh=mesh,
        in_specs=placed,
        out_specs=(P("shard", "rep", None), P("shard", None, None)),
        check_vma=False,
    )
```

profile of v0, /device:TPU:10, one launch (start us, length us, event | category | flops | bytes accessed | tf_op | source)
XLA Modules:
  0.0 153.2 jit_solution(7692912007405953353)
XLA Ops:
  0.6 2.8 %copy.9 = f32[16,1,64,256]{3,0,1,2:T(8,128)} copy(f32[16,1,64,256]{3,2,1,0:T(8,128)} %param.8) | data formatting | bytes 2097152 | tf_op args[0]
  3.5 9.3 %all-to-all-start = ((f32[16,1,64,256]{3,0,1,2:T(8,128)}), f32[16,1,64,256]{3,0,1,2:T(8,128)S(1)}, u32[]{:S(2)}, u32[]{:S(2)}) async-start(f32[16,1,64,256]{3,0,1,2:T(8,128)} %copy.9), calls=%async_computation | async-start | bytes 2097152 | tf_op jit(solution)/shard_map/all_to_all | solution.py:78
  13.3 92.7 %while.14 = (s32[]{:T(128)}, f32[512,1024]{1,0:T(8,128)S(1)}, s32[16384]{0:T(1024)}, s32[16384]{0:T(1024)}, s32[1024]{0:T(1024)S(1)}, /*index=5*/s32[1024]{0:T(1...) while((s32[]{:T(128)}, f32[512,1024]{1,0:T(8,128)S(1)}, s32[16384]{0:T(1024)}, s32[16384]{0:T(1024)}, ...), condition=%wide.region_3.4_spmd.clone, body=%wide.region_2.3_spmd.clone.sunk | while | flops 540279296 | bytes 4219049 | solution.py:63
  14.9 1.3 select_add_fusion.2
  17.8 1.3 select_add_fusion.2
  19.1 0.8 dynamic_slice.30
  20.7 1.3 select_add_fusion.2
  23.6 1.3 select_add_fusion.2
  26.5 1.3 select_add_fusion.2
  29.3 1.3 select_add_fusion.2
  30.7 0.8 dynamic_slice.30
  32.2 1.3 select_add_fusion.2
  33.6 0.8 dynamic_slice.30
  35.1 1.3 select_add_fusion.2
  36.5 0.8 dynamic_slice.30
  38.0 1.3 select_add_fusion.2
  39.4 0.8 dynamic_slice.30
  40.9 1.3 select_add_fusion.2
  43.8 1.3 select_add_fusion.2
  46.7 1.3 select_add_fusion.2
  49.6 1.3 select_add_fusion.2
  52.5 1.3 select_add_fusion.2
  55.4 1.3 select_add_fusion.2
  56.8 0.8 dynamic_slice.30
  58.3 1.3 select_add_fusion.2
  59.7 0.8 dynamic_slice.30
  61.2 1.3 select_add_fusion.2
  64.1 1.3 select_add_fusion.2
  67.0 1.3 select_add_fusion.2
  69.9 1.3 select_add_fusion.2
  72.8 1.3 select_add_fusion.2
  75.7 1.3 select_add_fusion.2
  78.6 1.3 select_add_fusion.2
  81.5 1.3 select_add_fusion.2
  84.4 1.3 select_add_fusion.2
  87.3 1.3 select_add_fusion.2
  90.2 1.3 select_add_fusion.2
  93.1 1.3 select_add_fusion.2
  96.0 1.3 select_add_fusion.2
  98.9 1.3 select_add_fusion.2
  101.8 1.3 select_add_fusion.2
  104.7 1.3 select_add_fusion.2
  106.0 2.6 %convolution_multiply_fusion = f32[512,256]{1,0:T(8,128)} fusion(f32[512,1024]{1,0:T(8,128)S(1)} %get-tuple-element.126, f32[1024,256]{1,0:T(8,128)S(1)} %bitcast.32), kind=kOutput, calls=%fused_computation.16 | convolution fusion | flops 1610743808 | bytes 3670016 | tf_op jit(solution)/shard_map/dot_general | solution.py:65
  108.6 7.6 %all-to-all-start.1 = ((f32[4,1,128,256]{3,2,1,0:T(8,128)}), f32[4,1,128,256]{3,2,1,0:T(8,128)S(1)}, u32[]{:S(2)}, u32[]{:S(2)}) async-start(f32[4,1,128,256]{3,2,1,0:T(8,128)} %bitcast.33), calls=%async_computation.1 | async-start | bytes 1048576 | tf_op jit(solution)/shard_map/all_to_all | solution.py:17
  116.2 14.1 %all-to-all-done.1 = f32[4,1,128,256]{3,2,1,0:T(8,128)S(1)} async-done(((f32[4,1,128,256]{3,2,1,0:T(8,128)}), f32[4,1,128,256]{3,2,1,0:T(8,128)S(1)}, u32[]{:S(2)}, u32[]{:S(2)}) %all-to-all-start.1) | async-done | bytes 524320 | tf_op jit(solution)/shard_map/all_to_all | solution.py:17
  131.1 1.0 subtract_bitcast_fusion
  132.1 20.3 %all_to_all.25 = f32[4,1,128,256]{3,2,1,0:T(8,128)S(1)} all-to-all(f32[4,1,128,256]{3,2,1,0:T(8,128)S(1)} %broadcast_in_dim.57), channel_id=1, replica_groups=mesh['shard'=64,'rep'=4] {'rep'}, dimensions={0} | all-to-all | bytes 1048576 | tf_op jit(solution)/shard_map/all_to_all | solution.py:23
  152.4 0.8 copy.18
  (104 shorter events, 45.0 us)
Async XLA Ops:
  0.6 12.1 %copy-start.1 = (s32[1,1,1024]{2,1,0:T(1,128)S(1)}, s32[1,1,1024]{2,1,0:T(1,128)}, u32[]{:S(2)}) copy-start(s32[1,1,1024]{2,1,0:T(1,128)} %param.9) | copy-start | bytes 12292
  3.5 102.6 %all-to-all-start = ((f32[16,1,64,256]{3,0,1,2:T(8,128)}), f32[16,1,64,256]{3,0,1,2:T(8,128)S(1)}, u32[]{:S(2)}, u32[]{:S(2)}) async-start(f32[16,1,64,256]{3,0,1,2:T(8,128)} %copy.9), calls=%async_computation | async-start | bytes 2097152 | tf_op jit(solution)/shard_map/all_to_all | solution.py:78
  108.6 21.6 %all-to-all-start.1 = ((f32[4,1,128,256]{3,2,1,0:T(8,128)}), f32[4,1,128,256]{3,2,1,0:T(8,128)S(1)}, u32[]{:S(2)}, u32[]{:S(2)}) async-start(f32[4,1,128,256]{3,2,1,0:T(8,128)} %bitcast.33), calls=%async_computation.1 | async-start | bytes 1048576 | tf_op jit(solution)/shard_map/all_to_all | solution.py:17
  130.3 22.9 %copy-start = (f32[128,256]{1,0:T(8,128)}, f32[128,256]{1,0:T(8,128)S(1)}, u32[]{:S(2)}) copy-start(f32[128,256]{1,0:T(8,128)S(1)} %reduce_sum.20) | copy-start | bytes 393220
where the time goes:
time: 156 us; the launch traced here: 153 us
  local copies, waits for them, and re-layouts  52.6 us (34%)
  matrix products  45.4 us (29%)
  blocking collectives  20.3 us (13%)
  starting transfers between devices  16.8 us (11%)
  waiting for transfers between devices  14.1 us (9%)
  other arithmetic  2.29 us (1%)
    dot_general x32, matrix products, add_block(): lax.dot_general(chosen, member, (((0,), (0,)), ((), ())), preferred_eleme...  42.8 us
    dynamic_slice x32, local copies, waits for them, and re-layouts, add_block(): factor = lax.dynamic_slice_in_dim(weights, start, span)  24.5 us
    dynamic_slice x32, local copies, waits for them, and re-layouts, add_block(): target = lax.dynamic_slice_in_dim(slots, start, span)  24.3 us
    all_to_all x1, blocking collectives, copy_for_each(): lax.all_to_all(jnp.broadcast_to(array[None], (count, *array.shape)), axis...  20.3 us
    all_to_all x1, waiting for transfers between devices, summed_on_arrival(): lax.all_to_all(pieces, axis, split_axis=0, concat_axis=0, tiled=True)  14.1 us
    all_to_all x1, starting transfers between devices, per_device(): lax.all_to_all(pooled_grad, 'shard', split_axis=2, concat_axis=0, tiled=T...  9.27 us
    all_to_all x1, starting transfers between devices, summed_on_arrival(): lax.all_to_all(pieces, axis, split_axis=0, concat_axis=0, tiled=True)  7.56 us
    unnamed x6, local copies, waits for them, and re-layouts  3.63 us
  transfers between devices with their start and end apart: 2, of which 1 were waited for; matrix products, arithmetic and copies ran while one was open for 60% of the time, Pallas kernels for 0%

commit v1 on v0

v1 whole, which is shorter than its diff:
```python
import jax
import jax.numpy as jnp
from jax import lax
from jax.experimental import pallas as pl
from jax.experimental.pallas import tpu as pltpu
from jax.sharding import PartitionSpec as P

learn_rate = 0.5
span = 512
window = 256
VMEM = pltpu.VMEM
SMEM = pltpu.SMEM


def tally_kernel(edges, starts_ref, ends_ref, slots_ref, weights_ref, high_ref, low_ref, total):
    height = total.shape[0]
    slot_ids = lax.broadcasted_iota(jnp.int32, (height, span), 0)
    offsets = lax.broadcasted_iota(jnp.int32, (span, window), 0)
    for part in range(high_ref.shape[1] // window):
        columns = pl.ds(part * window, window)
        starts = starts_ref[:, columns]
        ends = ends_ref[:, columns]
        total[...] = jnp.zeros_like(total)

        def add_block(block, carry):
            base = pl.multiple_of(block * span, span)
            slots = slots_ref[:, pl.ds(base, span)]
            weights = weights_ref[:, pl.ds(base, span)]
            chosen = jnp.where(slot_ids == slots, weights.astype(jnp.float32), 0.0)
            member = (offsets >= starts - base) & (offsets < ends - base)
            total[...] += jnp.dot(
                chosen.astype(jnp.bfloat16),
                jnp.where(member, 1.0, 0.0).astype(jnp.bfloat16),
                preferred_element_type=jnp.float32,
            )
            return carry

        first = edges[part] // span
        last = (edges[part + 1] + span - 1) // span
        lax.fori_loop(first, last, add_block, 0)
        high = total[...].astype(jnp.bfloat16)
        high_ref[:, columns] = high
        low_ref[:, columns] = (total[...] - high.astype(jnp.float32)).astype(jnp.bfloat16)


def tallies(lengths, slots, weights, height):
    bags = lengths.shape[1]
    ends = jnp.cumsum(lengths, axis=1)
    starts = ends - lengths
    edges = jnp.concatenate([starts[0, ::window], ends[0, -1:]])
    shape = jax.ShapeDtypeStruct((height, bags), jnp.bfloat16)
    return pl.pallas_call(
        tally_kernel,
        out_shape=(shape, shape),
        in_specs=[pl.BlockSpec(memory_space=SMEM)] + [pl.BlockSpec(memory_space=VMEM)] * 4,
        out_specs=(pl.BlockSpec(memory_space=VMEM),) * 2,
        scratch_shapes=[pltpu.VMEM((height, window), jnp.float32)],
        compiler_params=pltpu.CompilerParams(vmem_limit_bytes=24 << 20),
        cost_estimate=pl.CostEstimate(
            flops=2 * 35 * height * span * window, bytes_accessed=2 << 20, transcendentals=0
        ),
    )(edges, starts, ends, slots, weights)


def rows_kernel(picks, high_ref, low_ref, arrived_ref, out_ref):
    wide = arrived_ref[...]
    upper = wide.astype(jnp.bfloat16)
    lower = (wide - upper.astype(jnp.float32)).astype(jnp.bfloat16)
    count = out_ref.shape[1]
    for place in range(out_ref.shape[0]):
        rows = pl.ds(pl.multiple_of(picks[place] * count, count), count)
        high = high_ref[rows, :]
        low = low_ref[rows, :]
        dot = lambda a, b: jnp.dot(a, b, preferred_element_type=jnp.float32)
        out_ref[place] = (dot(high, lower) + dot(low, upper) + dot(high, upper)) * 0.0625


def grad_rows(picks, high, low, arrived, count):
    width = arrived.shape[1]
    return pl.pallas_call(
        rows_kernel,
        out_shape=jax.ShapeDtypeStruct((picks.shape[0], count, width), jnp.float32),
        in_specs=[pl.BlockSpec(memory_space=SMEM)] + [pl.BlockSpec(memory_space=VMEM)] * 3,
        out_specs=pl.BlockSpec(memory_space=VMEM),
        compiler_params=pltpu.CompilerParams(vmem_limit_bytes=24 << 20),
        cost_estimate=pl.CostEstimate(
            flops=6 * picks.shape[0] * count * width * high.shape[1],
            bytes_accessed=4 << 20,
            transcendentals=0,
        ),
    )(picks, high, low, arrived)


def adagrad_kernel(picks, mine_ref, other_ref, rows_ref, state_ref, grad_ref, fresh_ref):
    count = mine_ref.shape[1]
    for place in range(2):
        rows = pl.ds(pl.multiple_of(picks[place] * count, count), count)
        grads = mine_ref[place] + other_ref[1 - place]
        if place == 0:
            grad_ref[...] = grads
        state = state_ref[rows, :] + jnp.mean(grads * grads, axis=-1, keepdims=True)
        fresh_ref[place] = rows_ref[rows, :] - learn_rate * grads / (jnp.sqrt(state) + 1e-08)


def adagrad(picks, mine, other, rows, state):
    _, count, width = mine.shape
    return pl.pallas_call(
        adagrad_kernel,
        out_shape=(
            jax.ShapeDtypeStruct((count, width), jnp.float32),
            jax.ShapeDtypeStruct((2, count, width), jnp.float32),
        ),
        in_specs=[pl.BlockSpec(memory_space=SMEM)] + [pl.BlockSpec(memory_space=VMEM)] * 4,
        out_specs=(pl.BlockSpec(memory_space=VMEM),) * 2,
        compiler_params=pltpu.CompilerParams(vmem_limit_bytes=16 << 20),
    )(picks, mine, other, rows, state)


def per_device(pooled_grad, bag_lengths, row_slots, id_weights, touched_rows, accumulator):
    reps = lax.axis_size("rep")
    shards = lax.axis_size("shard")
    height = touched_rows.shape[1]
    count = height // reps
    rep = lax.axis_index("rep")
    core = lax.axis_index("shard") % 2
    near = jnp.where(core == 0, 1, 3)
    keep = jnp.stack([rep, rep ^ (near ^ 2)])
    give = jnp.stack([rep ^ near, rep ^ 2])

    def swap(array, step):
        pairs = []
        for shard in range(shards):
            turn = 1 if (shard + step) % 2 == 0 else 3
            pairs += [(shard * reps + r, shard * reps + (r ^ turn)) for r in range(reps)]
        return lax.ppermute(array, ("shard", "rep"), pairs)

    arrived = lax.all_to_all(pooled_grad, "shard", split_axis=2, concat_axis=0, tiled=True)
    arrived = arrived[:, 0, 0]
    high, low = tallies(bag_lengths[0], row_slots[0], id_weights[0], height)
    sent = swap(grad_rows(give, high, low, arrived, count), 0)
    mine = grad_rows(keep, high, low, arrived, count) + sent
    other = swap(mine, 1)
    grad, fresh = adagrad(keep, mine, other, touched_rows[0], accumulator.reshape(height, 1))
    far = swap(fresh, 0)
    updated = jnp.zeros((reps, count, touched_rows.shape[2]), jnp.float32)
    for place in range(2):
        updated = lax.dynamic_update_index_in_dim(updated, fresh[place], keep[place], 0)
    for place in range(2):
        updated = lax.dynamic_update_index_in_dim(updated, far[place], give[place], 0)
    return grad[None], updated.reshape(touched_rows.shape)


def solution(mesh):
    placed = (
        P("shard", "rep", None, None),
        P("shard", "rep", None),
        P("shard", "rep", None),
        P("shard", "rep", None),
        P("shard", None, None),
        P("shard", None),
    )
    return jax.shard_map(
        per_device,
        mesh=mesh,
        in_specs=placed,
        out_specs=(P("shard", "rep", None), P("shard", None, None)),
        check_vma=False,
    )
```

time: 156 us -> 69.4 us (0.44)
  the two profiles are of different devices: /device:TPU:10 before, /device:TPU:2 now
where the time goes in v1:
time: 69.4 us; the launch traced here: 69.1 us
  waiting for transfers between devices  23.4 us (34%)
  starting transfers between devices  17.3 us (25%)
  Pallas kernels  17.3 us (25%)
  local copies, waits for them, and re-layouts  7.97 us (11%)
  other arithmetic  2.33 us (3%)
  between operations  0.79 us (1%)
    ppermute x3, waiting for transfers between devices, swap(): return lax.ppermute(array, ('shard', 'rep'), pairs)  22.3 us
    pallas_call x1, Pallas kernels, tallies(): pl.pallas_call(tally_kernel, out_shape=(shape, shape), in_specs=[pl.Block...  13.8 us
    all_to_all x1, starting transfers between devices, per_device(): lax.all_to_all(pooled_grad, 'shard', split_axis=2, concat_axis=0, tiled=T...  9.7 us
    ppermute x3, starting transfers between devices, swap(): return lax.ppermute(array, ('shard', 'rep'), pairs)  7.63 us
    unnamed x13, local copies, waits for them, and re-layouts  4.35 us
    all_to_all x2, local copies, waits for them, and re-layouts, per_device(): lax.all_to_all(pooled_grad, 'shard', split_axis=2, concat_axis=0, tiled=T...  2.45 us
    pallas_call x2, Pallas kernels, grad_rows(): pl.pallas_call(rows_kernel, out_shape=jax.ShapeDtypeStruct((picks.shape[0...  2.25 us
  transfers between devices with their start and end apart: 4, of which 4 were waited for; matrix products, arithmetic and copies ran while one was open for 4% of the time, Pallas kernels for 22%

profile of v1, /device:TPU:2, one launch (start us, length us, event | category | flops | bytes accessed | tf_op | source)
XLA Modules:
  0.0 69.1 jit_solution(15242029732809216057)
XLA Ops:
  0.6 2.9 %copy.17 = f32[16,1,64,256]{3,0,1,2:T(8,128)} copy(f32[16,1,64,256]{3,2,1,0:T(8,128)} %param.6) | data formatting | bytes 2097152 | tf_op args[0]
  3.5 0.0 copy-start.4
  3.5 0.0 copy-start.2
  3.5 9.7 %all-to-all-start = ((f32[16,1,64,256]{3,0,1,2:T(8,128)}), f32[16,1,64,256]{3,0,1,2:T(8,128)}, u32[]{:S(2)}, u32[]{:S(2)}) async-start(f32[16,1,64,256]{3,0,1,2:T(8,128)} %copy.17), calls=%async_computation | async-start | bytes 2097152 | tf_op jit(solution)/shard_map/all_to_all | solution.py:137
  13.2 0.0 copy-start.1
  13.2 0.0 copy-done.4
  13.2 0.3 reduce-window.6
  13.5 0.2 slice_reduce_fusion
  13.7 0.2 reduce-window.9
  13.9 0.1 broadcast.13
  14.0 0.6 slice.32
  14.6 0.1 slice.26
  14.7 0.7 %pad_add_fusion.1.edges = s32[5]{0:T(128)S(1)} fusion(s32[1]{0:T(128)} %bitcast.8, s32[4]{0:T(128)S(1)} %bitcast.39), kind=kLoop, calls=%fused_computation.8 | loop fusion | flops 5 | bytes 40 | tf_op jit(solution)/shard_map/concatenate | solution.py:50
  15.4 0.1 pad_add_fusion.2.picks
  15.4 0.0 copy-done.2
  15.5 0.0 copy-done.1
  15.5 13.8 %shard_map.77 = (bf16[512,1024]{1,0:T(8,128)(2,1)S(1)}, bf16[512,1024]{1,0:T(8,128)(2,1)S(1)}) custom-call(s32[5]{0:T(128)S(1)} %pad_add_fusion.1.edges, s32[1,1024]{1,0:T(1,128)S(1)} %get-tuple-element.10.starts_ref, s32[1,1024]{1,0:T(1,128)S(1)} %get-tuple-element.11.ends_ref, s32[1,16384]{1,0:T(1,128)S(1)} %bitcast.29, s32[1,16384]{1,0:T(1,128)S(1)} %bitcast.30), custom_call_target="tpu_custom_call" | custom-call | flops 4697620480 | bytes 2097152 | tf_op jit(solution)/shard_map/pallas_call | solution.py:52
  29.2 1.1 %all-to-all-done = f32[16,1,64,256]{3,0,1,2:T(8,128)} async-done(((f32[16,1,64,256]{3,0,1,2:T(8,128)}), f32[16,1,64,256]{3,0,1,2:T(8,128)}, u32[]{:S(2)}, u32[]{:S(2)}) %all-to-all-start) | async-done | bytes 1048608 | tf_op jit(solution)/shard_map/all_to_all | solution.py:137
  30.3 1.8 %copy.22 = f32[16,1,64,256]{3,2,0,1:T(8,128)S(1)} copy(f32[16,1,64,256]{3,0,1,2:T(8,128)} %all-to-all-done) | data formatting | bytes 2097152 | tf_op jit(solution)/shard_map/all_to_all | solution.py:137
  32.1 0.6 copy.19
  32.7 1.1 %shard_map.79 = f32[2,128,256]{2,1,0:T(8,128)S(1)} custom-call(s32[2]{0:T(128)S(1)} %pad_add_fusion.2.picks, bf16[512,1024]{1,0:T(8,128)(2,1)S(1)} %get-tuple-element.6.high_ref, bf16[512,1024]{1,0:T(8,128)(2,1)S(1)} %get-tuple-element.7.low_ref, f32[1024,256]{1,0:T(8,128)S(1)} %bitcast.26), custom_call_target="tpu_custom_call" | custom-call | flops 402653184 | bytes 4194304 | tf_op jit(solution)/shard_map/pallas_call | solution.py:80
  33.9 3.4 %collective-permute-start = (f32[2,128,256]{2,1,0:T(8,128)S(1)}, f32[2,128,256]{2,1,0:T(8,128)}, u32[]{:S(2)}, u32[]{:S(2)}) collective-permute-start(f32[2,128,256]{2,1,0:T(8,128)S(1)} %shard_map.79), channel_id=1, source_target_pairs={{0,1},{1,0},{2,3},{3,2},{4,7},{5,6},{6,5},{7,4},{8,9},{9,8},{10,11... | collective-permute-start | bytes 786440 | tf_op jit(solution)/shard_map/ppermute | solution.py:135
  37.2 0.1 pad_add_fusion.picks
  37.3 1.1 %shard_map.78 = f32[2,128,256]{2,1,0:T(8,128)S(1)} custom-call(s32[2]{0:T(128)S(1)} %pad_add_fusion.picks, bf16[512,1024]{1,0:T(8,128)(2,1)S(1)} %get-tuple-element.6.high_ref, bf16[512,1024]{1,0:T(8,128)(2,1)S(1)} %get-tuple-element.7.low_ref, f32[1024,256]{1,0:T(8,128)S(1)} %bitcast.27), custom_call_target="tpu_custom_call" | custom-call | flops 402653184 | bytes 4194304 | tf_op jit(solution)/shard_map/pallas_call | solution.py:80
  38.4 0.0 copy-start
  38.4 6.0 %collective-permute-done = f32[2,128,256]{2,1,0:T(8,128)} collective-permute-done((f32[2,128,256]{2,1,0:T(8,128)S(1)}, f32[2,128,256]{2,1,0:T(8,128)}, u32[]{:S(2)}, u32[]{:S(2)}) %collective-permute-start) | collective-permute-done | bytes 262176 | tf_op jit(solution)/shard_map/ppermute | solution.py:135
  44.5 1.0 %add.21.mine_ref = f32[2,128,256]{2,1,0:T(8,128)S(1)} add(f32[2,128,256]{2,1,0:T(8,128)S(1)} %shard_map.78, f32[2,128,256]{2,1,0:T(8,128)} %collective-permute-done) | non-fusion elementwise | flops 65536 | bytes 786432 | tf_op jit(solution)/shard_map/add | solution.py:141
  45.4 3.3 %collective-permute-start.1 = (f32[2,128,256]{2,1,0:T(8,128)S(1)}, f32[2,128,256]{2,1,0:T(8,128)S(1)}, u32[]{:S(2)}, u32[]{:S(2)}) collective-permute-start(f32[2,128,256]{2,1,0:T(8,128)S(1)} %add.21.mine_ref), channel_id=1, source_target_pairs={{0,3},{1,2},{2,1},{3,0},{4,5},{5,4},{6,7},{7,6},{8,11},{9,10},{10,... | collective-permute-start | bytes 786440 | tf_op jit(solution)/shard_map/ppermute | solution.py:135
  48.7 0.0 copy-start.5
  48.7 0.7 copy-done.5
  49.4 0.1 copy.20.state_ref
  49.6 7.3 %collective-permute-done.1.other_ref = f32[2,128,256]{2,1,0:T(8,128)S(1)} collective-permute-done((f32[2,128,256]{2,1,0:T(8,128)S(1)}, f32[2,128,256]{2,1,0:T(8,128)S(1)}, u32[]{:S(2)}, u32[]{:S(2)}) %collective-permute-start.1) | collective-permute-done | bytes 262176 | tf_op jit(solution)/shard_map/ppermute | solution.py:135
  56.9 0.0 copy-done
  56.9 1.3 %shard_map.80 = (f32[128,256]{1,0:T(8,128)}, f32[2,128,256]{2,1,0:T(8,128)S(1)}) custom-call(s32[2]{0:T(128)S(1)} %pad_add_fusion.picks, f32[2,128,256]{2,1,0:T(8,128)S(1)} %add.21.mine_ref, f32[2,128,256]{2,1,0:T(8,128)S(1)} %collective-permute-done.1.other_ref, f32[512,256]{1,0:T(8,128)S(1)} %bitcast.28, f32[512,1]{1,0:T(8,128)S(1)} %copy.20.state_ref), custom_call_target="tpu_custom_call" | custom-call | tf_op jit(solution)/shard_map/pallas_call | solution.py:107
  58.1 1.0 %collective-permute-start.2 = (f32[2,128,256]{2,1,0:T(8,128)S(1)}, f32[2,128,256]{2,1,0:T(8,128)S(1)}, u32[]{:S(2)}, u32[]{:S(2)}) collective-permute-start(f32[2,128,256]{2,1,0:T(8,128)S(1)} %get-tuple-element.9), channel_id=1, source_target_pairs={{0,1},{1,0},{2,3},{3,2},{4,7},{5,6},{6,5},{7,4},{8,9},{9,8},{10,11... | collective-permute-start | bytes 786440 | tf_op jit(solution)/shard_map/ppermute | solution.py:135
  59.2 9.1 %collective-permute-done.2 = f32[2,128,256]{2,1,0:T(8,128)S(1)} collective-permute-done((f32[2,128,256]{2,1,0:T(8,128)S(1)}, f32[2,128,256]{2,1,0:T(8,128)S(1)}, u32[]{:S(2)}, u32[]{:S(2)}) %collective-permute-start.2) | collective-permute-done | bytes 262176 | tf_op jit(solution)/shard_map/ppermute | solution.py:135
  68.3 0.0 copy-start.3
  68.3 0.8 %copy-done.3 = f32[4,128,256]{2,1,0:T(8,128)} copy-done((f32[4,128,256]{2,1,0:T(8,128)}, f32[4,128,256]{2,1,0:T(8,128)S(1)}, u32[]{:S(2)}) %copy-start.3) | copy-done | bytes 524312
  (7 shorter events, 0.1 us)
Async XLA Ops:
  3.5 9.7 %copy-start.4 = (s32[1,1,1024]{2,1,0:T(1,128)S(1)}, s32[1,1,1024]{2,1,0:T(1,128)}, u32[]{:S(2)}) copy-start(s32[1,1,1024]{2,1,0:T(1,128)} %param.7) | copy-start | bytes 12292
  3.5 12.0 %copy-start.2 = (s32[1,1,16384]{2,1,0:T(1,128)S(1)}, s32[1,1,16384]{2,1,0:T(1,128)}, u32[]{:S(2)}) copy-start(s32[1,1,16384]{2,1,0:T(1,128)} %param.9) | copy-start | bytes 196612
  3.5 26.8 %all-to-all-start = ((f32[16,1,64,256]{3,0,1,2:T(8,128)}), f32[16,1,64,256]{3,0,1,2:T(8,128)}, u32[]{:S(2)}, u32[]{:S(2)}) async-start(f32[16,1,64,256]{3,0,1,2:T(8,128)} %copy.17), calls=%async_computation | async-start | bytes 2097152 | tf_op jit(solution)/shard_map/all_to_all | solution.py:137
  13.2 2.3 %copy-start.1 = (s32[1,1,16384]{2,1,0:T(1,128)S(1)}, s32[1,1,16384]{2,1,0:T(1,128)}, u32[]{:S(2)}) copy-start(s32[1,1,16384]{2,1,0:T(1,128)} %param.8) | copy-start | bytes 196612
  33.9 10.6 %collective-permute-start = (f32[2,128,256]{2,1,0:T(8,128)S(1)}, f32[2,128,256]{2,1,0:T(8,128)}, u32[]{:S(2)}, u32[]{:S(2)}) collective-permute-start(f32[2,128,256]{2,1,0:T(8,128)S(1)} %shard_map.79), channel_id=1, source_target_pairs={{0,1},{1,0},{2,3},{3,2},{4,7},{5,6},{6,5},{7,4},{8,9},{9,8},{10,11... | collective-permute-start | bytes 786440 | tf_op jit(solution)/shard_map/ppermute | solution.py:135
  38.4 18.4 %copy-start = (f32[1,512,256]{2,1,0:T(8,128)S(1)}, f32[1,512,256]{2,1,0:T(8,128)}, u32[]{:S(2)}) copy-start(f32[1,512,256]{2,1,0:T(8,128)} %param.10) | copy-start | bytes 1572868
  45.4 11.4 %collective-permute-start.1 = (f32[2,128,256]{2,1,0:T(8,128)S(1)}, f32[2,128,256]{2,1,0:T(8,128)S(1)}, u32[]{:S(2)}, u32[]{:S(2)}) collective-permute-start(f32[2,128,256]{2,1,0:T(8,128)S(1)} %add.21.mine_ref), channel_id=1, source_target_pairs={{0,3},{1,2},{2,1},{3,0},{4,5},{5,4},{6,7},{7,6},{8,11},{9,10},{10,... | collective-permute-start | bytes 786440 | tf_op jit(solution)/shard_map/ppermute | solution.py:135
  48.7 0.7 copy-start.5
  58.1 10.1 %collective-permute-start.2 = (f32[2,128,256]{2,1,0:T(8,128)S(1)}, f32[2,128,256]{2,1,0:T(8,128)S(1)}, u32[]{:S(2)}, u32[]{:S(2)}) collective-permute-start(f32[2,128,256]{2,1,0:T(8,128)S(1)} %get-tuple-element.9), channel_id=1, source_target_pairs={{0,1},{1,0},{2,3},{3,2},{4,7},{5,6},{6,5},{7,4},{8,9},{9,8},{10,11... | collective-permute-start | bytes 786440 | tf_op jit(solution)/shard_map/ppermute | solution.py:135
  68.3 0.8 %copy-start.3 = (f32[4,128,256]{2,1,0:T(8,128)}, f32[4,128,256]{2,1,0:T(8,128)S(1)}, u32[]{:S(2)}) copy-start(f32[4,128,256]{2,1,0:T(8,128)S(1)} %slice_dynamic-update-slice_fusion) | copy-start | bytes 1572868

commit v2 on v1

v2 whole, which is shorter than its diff:
```python
import jax
import jax.numpy as jnp
from jax import lax
from jax.experimental import pallas as pl
from jax.experimental.pallas import tpu as pltpu
from jax.sharding import PartitionSpec as P

learn_rate = 0.5
span = 1024
block = 256
window = 256
VMEM = pltpu.VMEM
SMEM = pltpu.SMEM


def tally_kernel(edges, starts_ref, ends_ref, slots_ref, weights_ref, high_ref, low_ref, total):
    height = total.shape[0]
    narrow = jnp.bfloat16
    half = height // 2

    def coded(slots):
        return jnp.where(slots < half, slots, half - 1 - slots).astype(jnp.float32).astype(narrow)

    slot_ids = coded(lax.broadcasted_iota(jnp.int32, (height, block), 0))
    offsets = lax.broadcasted_iota(jnp.int32, (block, window), 0).astype(jnp.float32).astype(narrow)
    zero = jnp.zeros((), narrow)
    one = jnp.ones((), narrow)
    for part in range(high_ref.shape[1] // window):
        columns = pl.ds(part * window, window)
        starts = starts_ref[:, columns]
        ends = ends_ref[:, columns]
        total[...] = jnp.zeros_like(total)

        def add_span(step, carry):
            added = jnp.zeros_like(total)
            for piece in range(span // block):
                base = pl.multiple_of(step * span + piece * block, block)

                def local(bounds):
                    return jnp.clip(bounds - base, 0, block).astype(jnp.float32).astype(narrow)

                codes = coded(slots_ref[:, pl.ds(base, block)])
                weights = weights_ref[:, pl.ds(base, block)].astype(jnp.float32).astype(narrow)
                chosen = jnp.where(slot_ids == codes, weights, zero)
                member = (offsets >= local(starts)) & (offsets < local(ends))
                added += jnp.dot(
                    chosen, jnp.where(member, one, zero), preferred_element_type=jnp.float32
                )
            total[...] += added
            return carry

        first = edges[part] // span
        last = (edges[part + 1] + span - 1) // span
        lax.fori_loop(first, last, add_span, 0)
        high = total[...].astype(narrow)
        high_ref[:, columns] = high
        low_ref[:, columns] = (total[...] - high.astype(jnp.float32)).astype(narrow)


def spec(space):
    return pl.BlockSpec(memory_space=space)


def limit(mebibytes):
    return pltpu.CompilerParams(vmem_limit_bytes=mebibytes << 20)


def tallies(lengths, slots, weights, height):
    bags = lengths.shape[1]
    ends = jnp.cumsum(lengths, axis=1)
    starts = ends - lengths
    edges = jnp.concatenate([starts[0, ::window], ends[0, -1:]])
    shape = jax.ShapeDtypeStruct((height, bags), jnp.bfloat16)
    return pl.pallas_call(
        tally_kernel,
        out_shape=(shape, shape),
        in_specs=[spec(SMEM)] + [spec(VMEM)] * 4,
        out_specs=(spec(VMEM),) * 2,
        scratch_shapes=[pltpu.VMEM((height, window), jnp.float32)],
        compiler_params=limit(10),
        cost_estimate=pl.CostEstimate(
            flops=2 * 35 * height * 512 * window, bytes_accessed=2 << 20, transcendentals=0
        ),
    )(edges, starts, ends, slots, weights)


def rows_kernel(picks, high_ref, low_ref, arrived_ref, *out_refs):
    wide = arrived_ref[...]
    upper = wide.astype(jnp.bfloat16)
    lower = (wide - upper.astype(jnp.float32)).astype(jnp.bfloat16)
    dot = lambda a, b: jnp.dot(a, b, preferred_element_type=jnp.float32)
    for place, out_ref in enumerate(out_refs):
        count = out_ref.shape[0]
        rows = pl.ds(pl.multiple_of(picks[place] * count, count), count)
        high = high_ref[rows, :]
        low = low_ref[rows, :]
        out_ref[...] = (dot(high, lower) + dot(low, upper) + dot(high, upper)) * 0.0625


def grad_rows(picks, high, low, arrived, count):
    width = arrived.shape[1]
    shape = jax.ShapeDtypeStruct((count, width), jnp.float32)
    return pl.pallas_call(
        rows_kernel,
        out_shape=(shape, shape),
        in_specs=[spec(SMEM)] + [spec(VMEM)] * 3,
        out_specs=(spec(VMEM),) * 2,
        compiler_params=limit(10),
        cost_estimate=pl.CostEstimate(
            flops=12 * count * width * high.shape[1], bytes_accessed=3 << 20, transcendentals=0
        ),
    )(picks, high, low, arrived)


def add_kernel(one_ref, two_ref, out_ref):
    out_ref[...] = one_ref[...] + two_ref[...]


def added(one, two):
    return pl.pallas_call(
        add_kernel,
        out_shape=jax.ShapeDtypeStruct(one.shape, one.dtype),
        in_specs=[spec(VMEM)] * 2,
        out_specs=spec(VMEM),
        compiler_params=limit(2),
    )(one, two)


def adagrad_kernel(pick, mine_ref, other_ref, rows_ref, state_ref, grad_ref, fresh_ref):
    count = mine_ref.shape[0]
    rows = pl.ds(pl.multiple_of(pick[0] * count, count), count)
    grads = mine_ref[...] + other_ref[...]
    grad_ref[...] = grads
    state = state_ref[rows, :] + jnp.mean(grads * grads, axis=-1, keepdims=True)
    fresh_ref[...] = rows_ref[rows, :] - learn_rate * grads / (jnp.sqrt(state) + 1e-08)


def adagrad(pick, mine, other, rows, state):
    shape = jax.ShapeDtypeStruct(mine.shape, jnp.float32)
    return pl.pallas_call(
        adagrad_kernel,
        out_shape=(shape, shape),
        in_specs=[spec(SMEM)] + [spec(VMEM)] * 4,
        out_specs=(spec(VMEM),) * 2,
        compiler_params=limit(4),
    )(pick, mine, other, rows, state)


def per_device(pooled_grad, bag_lengths, row_slots, id_weights, touched_rows, accumulator):
    reps = lax.axis_size("rep")
    shards = lax.axis_size("shard")
    height = touched_rows.shape[1]
    count = height // reps
    rep = lax.axis_index("rep")
    core = lax.axis_index("shard") % 2
    near = jnp.where(core == 0, 1, 3)

    def ordered(one, two):
        return jnp.stack([jnp.minimum(one, two), jnp.maximum(one, two)])

    keep = ordered(rep, rep ^ (near ^ 2))
    give = ordered(rep ^ near, rep ^ 2)

    def swap(array, step):
        pairs = []
        for shard in range(shards):
            turn = 1 if (shard + step) % 2 == 0 else 3
            pairs += [(shard * reps + r, shard * reps + (r ^ turn)) for r in range(reps)]
        return lax.ppermute(array, ("shard", "rep"), pairs)

    by_table = jnp.transpose(pooled_grad[:, 0], (1, 0, 2))
    arrived = lax.all_to_all(by_table, "shard", 0, 0, tiled=True)
    arrived = arrived.reshape(-1, arrived.shape[2])
    high, low = tallies(bag_lengths[0], row_slots[0], id_weights[0], height)
    state = accumulator.reshape(height, 1)
    given = grad_rows(give, high, low, arrived, count)
    sent = [swap(piece, 0) for piece in given]
    kept = grad_rows(keep, high, low, arrived, count)
    mine = [added(kept[k], sent[k]) for k in range(2)]
    other = [swap(piece, 1) for piece in mine]
    grads, fresh = zip(
        *[adagrad(keep[k : k + 1], mine[k], other[k], touched_rows[0], state) for k in range(2)]
    )
    far = [swap(piece, 0) for piece in fresh]
    grad = jnp.where(rep == keep[0], grads[0], grads[1])
    updated = jnp.zeros((reps, count, touched_rows.shape[2]), jnp.float32)
    for k in range(2):
        updated = lax.dynamic_update_index_in_dim(updated, fresh[k], keep[k], 0)
    for k in range(2):
        updated = lax.dynamic_update_index_in_dim(updated, far[k], give[k], 0)
    return grad[None], updated.reshape(touched_rows.shape)


def solution(mesh):
    placed = (
        P("shard", "rep", None, None),
        P("shard", "rep", None),
        P("shard", "rep", None),
        P("shard", "rep", None),
        P("shard", None, None),
        P("shard", None),
    )
    return jax.shard_map(
        per_device,
        mesh=mesh,
        in_specs=placed,
        out_specs=(P("shard", "rep", None), P("shard", None, None)),
        check_vma=False,
    )
```

time: 69.4 us -> 62.6 us (0.902)
  the two profiles are of different devices: /device:TPU:2 before, /device:TPU:10 now
where the time goes in v2:
time: 62.6 us; the launch traced here: 62.3 us
  starting transfers between devices  25.1 us (40%)
  waiting for transfers between devices  16.3 us (26%)
  Pallas kernels  12.5 us (20%)
  local copies, waits for them, and re-layouts  5.56 us (9%)
  other arithmetic  1.99 us (3%)
  between operations  0.84 us (1%)
    ppermute x6, starting transfers between devices, swap(): return lax.ppermute(array, ('shard', 'rep'), pairs)  15.7 us
    ppermute x6, waiting for transfers between devices, swap(): return lax.ppermute(array, ('shard', 'rep'), pairs)  12.2 us
    pallas_call x1, Pallas kernels, tallies(): pl.pallas_call(tally_kernel, out_shape=(shape, shape), in_specs=[spec(SME...  9.8 us
    all_to_all x1, starting transfers between devices, per_device(): arrived = lax.all_to_all(by_table, 'shard', 0, 0, tiled=True)  9.4 us
    unnamed x13, local copies, waits for them, and re-layouts  4.3 us
    all_to_all x1, waiting for transfers between devices, per_device(): arrived = lax.all_to_all(by_table, 'shard', 0, 0, tiled=True)  4.16 us
    pallas_call x2, Pallas kernels, grad_rows(): pl.pallas_call(rows_kernel, out_shape=(shape, shape), in_specs=[spec(SMEM...  2.26 us
  transfers between devices with their start and end apart: 7, of which 4 were waited for; matrix products, arithmetic and copies ran while one was open for 5% of the time, Pallas kernels for 18%

profile of v2, /device:TPU:10, one launch (start us, length us, event | category | flops | bytes accessed | tf_op | source)
XLA Modules:
  0.0 62.3 jit_solution(3943175284157752228)
XLA Ops:
  0.6 2.8 %copy.16 = f32[16,1,64,256]{3,0,2,1:T(8,128)} copy(f32[16,1,64,256]{3,2,1,0:T(8,128)} %param.6) | data formatting | bytes 2097152 | tf_op args[0]
  3.4 0.0 copy-start.4
  3.4 0.0 copy-start.2
  3.4 9.4 %all-to-all-start = ((f32[64,16,256]{2,1,0:T(8,128)}), f32[64,16,256]{2,1,0:T(8,128)S(1)}, u32[]{:S(2)}, u32[]{:S(2)}) async-start(f32[64,16,256]{2,1,0:T(8,128)} %bitcast.34), calls=%async_computation | async-start | bytes 2097152 | tf_op jit(solution)/shard_map/all_to_all | solution.py:172
  12.9 0.0 copy-start.1
  12.9 0.0 copy-done.4
  12.9 0.3 reduce-window.6
  13.2 0.2 slice_reduce_fusion
  13.4 0.2 reduce-window.9
  13.6 0.1 broadcast.13
  13.6 0.1 slice.14
  13.7 0.7 %slice.16 = s32[1,1]{1,0:T(1,128)} slice(s32[1,1024]{1,0:T(1,128)S(1)} %get-tuple-element.23.ends_ref), slice={[0:1], [1023:1024]} | slice | bytes 8 | tf_op jit(solution)/shard_map/slice | solution.py:72
  14.4 0.8 %pad_add_fusion.1.edges = s32[5]{0:T(128)S(1)} fusion(s32[1]{0:T(128)} %bitcast.8, s32[4]{0:T(128)S(1)} %bitcast.47), kind=kLoop, calls=%fused_computation.9 | loop fusion | flops 5 | bytes 40 | tf_op jit(solution)/shard_map/concatenate | solution.py:72
  15.2 0.1 pad_add_fusion
  15.2 0.0 copy-done.2
  15.2 0.0 copy-done.1
  15.3 9.8 %shard_map.77 = (bf16[512,1024]{1,0:T(8,128)(2,1)S(1)}, bf16[512,1024]{1,0:T(8,128)(2,1)S(1)}) custom-call(s32[5]{0:T(128)S(1)} %pad_add_fusion.1.edges, s32[1,1024]{1,0:T(1,128)S(1)} %get-tuple-element.22.starts_ref, s32[1,1024]{1,0:T(1,128)S(1)} %get-tuple-element.23.ends_ref, s32[1,16384]{1,0:T(1,128)S(1)} %bitcast.39, s32[1,16384]{1,0:T(1,128)S(1)} %bitcast.40), custom_call_target="tpu_custom_call" | custom-call | flops 4697620480 | bytes 2097152 | tf_op jit(solution)/shard_map/pallas_call | solution.py:74
  25.1 4.2 %all-to-all-done = f32[64,16,256]{2,1,0:T(8,128)S(1)} async-done(((f32[64,16,256]{2,1,0:T(8,128)}), f32[64,16,256]{2,1,0:T(8,128)S(1)}, u32[]{:S(2)}, u32[]{:S(2)}) %all-to-all-start) | async-done | bytes 1048608 | tf_op jit(solution)/shard_map/all_to_all | solution.py:172
  29.2 1.1 %shard_map.79 = (f32[128,256]{1,0:T(8,128)S(1)}, f32[128,256]{1,0:T(8,128)S(1)}) custom-call(s32[2]{0:T(128)S(1)} %get-tuple-element.25.picks, bf16[512,1024]{1,0:T(8,128)(2,1)S(1)} %get-tuple-element.12.high_ref, bf16[512,1024]{1,0:T(8,128)(2,1)S(1)} %get-tuple-element.13.low_ref, f32[1024,256]{1,0:T(8,128)S(1)} %bitcast.35), custom_call_target="tpu_custom_call" | custom-call | flops 402653184 | bytes 3145728 | tf_op jit(solution)/shard_map/pallas_call | solution.py:103
  30.4 3.4 %collective-permute-start = (f32[128,256]{1,0:T(8,128)S(1)}, f32[128,256]{1,0:T(8,128)S(1)}, u32[]{:S(2)}, u32[]{:S(2)}) collective-permute-start(f32[128,256]{1,0:T(8,128)S(1)} %get-tuple-element.15), channel_id=1, source_target_pairs={{0,1},{1,0},{2,3},{3,2},{4,7},{5,6},{6,5},{7,4},{8,9},{9,8},{10,11... | collective-permute-start | bytes 393224 | tf_op jit(solution)/shard_map/ppermute | solution.py:169
  33.7 0.1 collective-permute-start.2
  33.8 1.1 %shard_map.78 = (f32[128,256]{1,0:T(8,128)S(1)}, f32[128,256]{1,0:T(8,128)S(1)}) custom-call(s32[2]{0:T(128)S(1)} %get-tuple-element.24.picks, bf16[512,1024]{1,0:T(8,128)(2,1)S(1)} %get-tuple-element.12.high_ref, bf16[512,1024]{1,0:T(8,128)(2,1)S(1)} %get-tuple-element.13.low_ref, f32[1024,256]{1,0:T(8,128)S(1)} %bitcast.36), custom_call_target="tpu_custom_call" | custom-call | flops 402653184 | bytes 3145728 | tf_op jit(solution)/shard_map/pallas_call | solution.py:103
  34.9 2.5 %collective-permute-done.two_ref = f32[128,256]{1,0:T(8,128)S(1)} collective-permute-done((f32[128,256]{1,0:T(8,128)S(1)}, f32[128,256]{1,0:T(8,128)S(1)}, u32[]{:S(2)}, u32[]{:S(2)}) %collective-permute-start) | collective-permute-done | bytes 131104 | tf_op jit(solution)/shard_map/ppermute | solution.py:169
  37.4 0.0 copy-start
  37.5 6.6 %collective-permute-start.1 = (f32[128,256]{1,0:T(8,128)S(1)}, f32[128,256]{1,0:T(8,128)S(1)}, u32[]{:S(2)}, u32[]{:S(2)}) collective-permute-start(f32[128,256]{1,0:T(8,128)S(1)} %shard_map.80.mine_ref), channel_id=1, source_target_pairs={{0,3},{1,2},{2,1},{3,0},{4,5},{5,4},{6,7},{7,6},{8,11},{9,10},{10,... | collective-permute-start | bytes 393224 | tf_op jit(solution)/shard_map/ppermute | solution.py:169
  44.1 0.0 collective-permute-done.2.two_ref
  44.1 3.1 %collective-permute-start.3 = (f32[128,256]{1,0:T(8,128)S(1)}, f32[128,256]{1,0:T(8,128)S(1)}, u32[]{:S(2)}, u32[]{:S(2)}) collective-permute-start(f32[128,256]{1,0:T(8,128)S(1)} %shard_map.82.mine_ref), channel_id=1, source_target_pairs={{0,3},{1,2},{2,1},{3,0},{4,5},{5,4},{6,7},{7,6},{8,11},{9,10},{10,... | collective-permute-start | bytes 393224 | tf_op jit(solution)/shard_map/ppermute | solution.py:169
  47.2 0.0 copy-start.5
  47.2 0.7 %copy-done.5 = f32[1,512]{1,0:T(1,128)S(1)} copy-done((f32[1,512]{1,0:T(1,128)S(1)}, f32[1,512]{1,0:T(1,128)}, u32[]{:S(2)}) %copy-start.5) | copy-done | bytes 2072
  47.9 0.1 copy.13.state_ref
  48.0 0.0 collective-permute-done.1.other_ref
  48.1 0.0 copy-done
  48.1 0.2 shard_map.81
  48.3 2.4 %collective-permute-start.4 = (f32[128,256]{1,0:T(8,128)S(1)}, f32[128,256]{1,0:T(8,128)S(1)}, u32[]{:S(2)}, u32[]{:S(2)}) collective-permute-start(f32[128,256]{1,0:T(8,128)S(1)} %get-tuple-element.20), channel_id=1, source_target_pairs={{0,1},{1,0},{2,3},{3,2},{4,7},{5,6},{6,5},{7,4},{8,9},{9,8},{10,11... | collective-permute-start | bytes 393224 | tf_op jit(solution)/shard_map/ppermute | solution.py:169
  50.7 4.2 %collective-permute-done.3.other_ref = f32[128,256]{1,0:T(8,128)S(1)} collective-permute-done((f32[128,256]{1,0:T(8,128)S(1)}, f32[128,256]{1,0:T(8,128)S(1)}, u32[]{:S(2)}, u32[]{:S(2)}) %collective-permute-start.3) | collective-permute-done | bytes 131104 | tf_op jit(solution)/shard_map/ppermute | solution.py:169
  54.9 0.2 shard_map.83
  55.1 0.1 collective-permute-start.5
  55.3 0.7 %select_bitcast_fusion = f32[1,128,256]{2,1,0:T(8,128)} fusion(f32[128,256]{1,0:T(8,128)S(1)} %get-tuple-element.16, f32[128,256]{1,0:T(8,128)S(1)} %get-tuple-element.19, pred[]{:T(512)S(6)} %eq.9), kind=kLoop, calls=%fused_computation.5 | loop fusion | flops 32768 | bytes 393217 | tf_op jit(solution)/shard_map/broadcast_in_dim | solution.py:191
  56.0 0.0 collective-permute-done.4
  56.0 5.5 %collective-permute-done.5 = f32[128,256]{1,0:T(8,128)S(1)} collective-permute-done((f32[128,256]{1,0:T(8,128)S(1)}, f32[128,256]{1,0:T(8,128)S(1)}, u32[]{:S(2)}, u32[]{:S(2)}) %collective-permute-start.5) | collective-permute-done | bytes 131104 | tf_op jit(solution)/shard_map/ppermute | solution.py:169
  61.5 0.0 copy-start.3
  61.5 0.8 %copy-done.3 = f32[4,128,256]{2,1,0:T(8,128)} copy-done((f32[4,128,256]{2,1,0:T(8,128)}, f32[4,128,256]{2,1,0:T(8,128)S(1)}, u32[]{:S(2)}) %copy-start.3) | copy-done | bytes 524312
  (9 shorter events, 0.1 us)
Async XLA Ops:
  3.4 9.5 %copy-start.4 = (s32[1,1,1024]{2,1,0:T(1,128)S(1)}, s32[1,1,1024]{2,1,0:T(1,128)}, u32[]{:S(2)}) copy-start(s32[1,1,1024]{2,1,0:T(1,128)} %param.7) | copy-start | bytes 12292
  3.4 11.8 %copy-start.2 = (s32[1,1,16384]{2,1,0:T(1,128)S(1)}, s32[1,1,16384]{2,1,0:T(1,128)}, u32[]{:S(2)}) copy-start(s32[1,1,16384]{2,1,0:T(1,128)} %param.9) | copy-start | bytes 196612
  3.4 25.8 %all-to-all-start = ((f32[64,16,256]{2,1,0:T(8,128)}), f32[64,16,256]{2,1,0:T(8,128)S(1)}, u32[]{:S(2)}, u32[]{:S(2)}) async-start(f32[64,16,256]{2,1,0:T(8,128)} %bitcast.34), calls=%async_computation | async-start | bytes 2097152 | tf_op jit(solution)/shard_map/all_to_all | solution.py:172
  12.9 2.4 %copy-start.1 = (s32[1,1,16384]{2,1,0:T(1,128)S(1)}, s32[1,1,16384]{2,1,0:T(1,128)}, u32[]{:S(2)}) copy-start(s32[1,1,16384]{2,1,0:T(1,128)} %param.8) | copy-start | bytes 196612
  30.4 7.1 %collective-permute-start = (f32[128,256]{1,0:T(8,128)S(1)}, f32[128,256]{1,0:T(8,128)S(1)}, u32[]{:S(2)}, u32[]{:S(2)}) collective-permute-start(f32[128,256]{1,0:T(8,128)S(1)} %get-tuple-element.15), channel_id=1, source_target_pairs={{0,1},{1,0},{2,3},{3,2},{4,7},{5,6},{6,5},{7,4},{8,9},{9,8},{10,11... | collective-permute-start | bytes 393224 | tf_op jit(solution)/shard_map/ppermute | solution.py:169
  33.7 10.3 %collective-permute-start.2 = (f32[128,256]{1,0:T(8,128)S(1)}, f32[128,256]{1,0:T(8,128)S(1)}, u32[]{:S(2)}, u32[]{:S(2)}) collective-permute-start(f32[128,256]{1,0:T(8,128)S(1)} %get-tuple-element.18), channel_id=1, source_target_pairs={{0,1},{1,0},{2,3},{3,2},{4,7},{5,6},{6,5},{7,4},{8,9},{9,8},{10,11... | collective-permute-start | bytes 393224 | tf_op jit(solution)/shard_map/ppermute | solution.py:169
  37.4 10.6 %copy-start = (f32[1,512,256]{2,1,0:T(8,128)S(1)}, f32[1,512,256]{2,1,0:T(8,128)}, u32[]{:S(2)}) copy-start(f32[1,512,256]{2,1,0:T(8,128)} %param.10) | copy-start | bytes 1572868
  37.5 10.6 %collective-permute-start.1 = (f32[128,256]{1,0:T(8,128)S(1)}, f32[128,256]{1,0:T(8,128)S(1)}, u32[]{:S(2)}, u32[]{:S(2)}) collective-permute-start(f32[128,256]{1,0:T(8,128)S(1)} %shard_map.80.mine_ref), channel_id=1, source_target_pairs={{0,3},{1,2},{2,1},{3,0},{4,5},{5,4},{6,7},{7,6},{8,11},{9,10},{10,... | collective-permute-start | bytes 393224 | tf_op jit(solution)/shard_map/ppermute | solution.py:169
  44.1 10.8 %collective-permute-start.3 = (f32[128,256]{1,0:T(8,128)S(1)}, f32[128,256]{1,0:T(8,128)S(1)}, u32[]{:S(2)}, u32[]{:S(2)}) collective-permute-start(f32[128,256]{1,0:T(8,128)S(1)} %shard_map.82.mine_ref), channel_id=1, source_target_pairs={{0,3},{1,2},{2,1},{3,0},{4,5},{5,4},{6,7},{7,6},{8,11},{9,10},{10,... | collective-permute-start | bytes 393224 | tf_op jit(solution)/shard_map/ppermute | solution.py:169
  47.2 0.7 %copy-start.5 = (f32[1,512]{1,0:T(1,128)S(1)}, f32[1,512]{1,0:T(1,128)}, u32[]{:S(2)}) copy-start(f32[1,512]{1,0:T(1,128)} %param.11) | copy-start | bytes 6148
  48.3 7.7 %collective-permute-start.4 = (f32[128,256]{1,0:T(8,128)S(1)}, f32[128,256]{1,0:T(8,128)S(1)}, u32[]{:S(2)}, u32[]{:S(2)}) collective-permute-start(f32[128,256]{1,0:T(8,128)S(1)} %get-tuple-element.20), channel_id=1, source_target_pairs={{0,1},{1,0},{2,3},{3,2},{4,7},{5,6},{6,5},{7,4},{8,9},{9,8},{10,11... | collective-permute-start | bytes 393224 | tf_op jit(solution)/shard_map/ppermute | solution.py:169
  55.1 6.4 %collective-permute-start.5 = (f32[128,256]{1,0:T(8,128)S(1)}, f32[128,256]{1,0:T(8,128)S(1)}, u32[]{:S(2)}, u32[]{:S(2)}) collective-permute-start(f32[128,256]{1,0:T(8,128)S(1)} %get-tuple-element.21), channel_id=1, source_target_pairs={{0,1},{1,0},{2,3},{3,2},{4,7},{5,6},{6,5},{7,4},{8,9},{9,8},{10,11... | collective-permute-start | bytes 393224 | tf_op jit(solution)/shard_map/ppermute | solution.py:169
  61.5 0.8 %copy-start.3 = (f32[4,128,256]{2,1,0:T(8,128)}, f32[4,128,256]{2,1,0:T(8,128)S(1)}, u32[]{:S(2)}) copy-start(f32[4,128,256]{2,1,0:T(8,128)S(1)} %bitcast_dynamic-update-slice_fusion) | copy-start | bytes 1572868

commit v3 on v2

--- a/solution.py
+++ b/solution.py
@@ -84,32 +84,111 @@
     )(edges, starts, ends, slots, weights)
 
 
-def rows_kernel(picks, high_ref, low_ref, arrived_ref, *out_refs):
+def by_table_kernel(samples_ref, tables_ref, taken, placed, in_sems, out_sems):
+    steps, _, each, lanes = taken.shape
+    halves = 2
+    groups = steps // halves
+    count = placed.shape[1]
+
+    def fetch(step):
+        group, half = step // halves, step % halves
+        rows = samples_ref.at[:, 0, pl.ds(each * group, each), pl.ds(lanes * half, lanes)]
+        return pltpu.make_async_copy(rows, taken.at[step], in_sems.at[step])
+
+    def put(group):
+        tables = pl.ds(each * group, each)
+        return pltpu.make_async_copy(placed.at[tables], tables_ref.at[tables], out_sems.at[group])
+
+    for step in range(steps):
+        fetch(step).start()
+    for step in range(steps):
+        group, half = step // halves, step % halves
+        fetch(step).wait()
+        rows = taken.at[step].reshape(count * each, lanes)
+        for table in range(each):
+            picked = rows[pl.ds(table, count, stride=each), :]
+            placed[each * group + table, :, lanes * half : lanes * (half + 1)] = picked
+        if half == halves - 1:
+            put(group).start()
+    for group in range(groups):
+        put(group).wait()
+
+
+def by_table(samples):
+    count, _, tables, width = samples.shape
+    groups, lanes = tables // 8, width // 2
+    return pl.pallas_call(
+        by_table_kernel,
+        out_shape=jax.ShapeDtypeStruct((tables, count, width), jnp.float32),
+        in_specs=[spec(pltpu.HBM)],
+        out_specs=spec(pltpu.HBM),
+        scratch_shapes=[
+            pltpu.VMEM((2 * groups, count, 8, lanes), jnp.float32),
+            pltpu.VMEM((tables, count, width), jnp.float32),
+            pltpu.SemaphoreType.DMA((2 * groups,)),
+            pltpu.SemaphoreType.DMA((groups,)),
+        ],
+        compiler_params=limit(63),
+    )(samples)
+
+
+def chunk_rows(place, high_ref, low_ref, upper, lower, count):
+    rows = pl.ds(pl.multiple_of(place * count, count), count)
+    high = high_ref[rows, :]
+    low = low_ref[rows, :]
+    dot = lambda a, b: jnp.dot(a, b, preferred_element_type=jnp.float32)
+    both = dot(jnp.concatenate([high, low]), upper)
+    return (dot(high, lower) + both[count:] + both[:count]) * 0.0625
+
+
+def first_kernel(picks, high_ref, low_ref, arrived_ref, upper_ref, lower_ref, *out_refs):
     wide = arrived_ref[...]
     upper = wide.astype(jnp.bfloat16)
     lower = (wide - upper.astype(jnp.float32)).astype(jnp.bfloat16)
-    dot = lambda a, b: jnp.dot(a, b, preferred_element_type=jnp.float32)
+    upper_ref[...] = upper
+    lower_ref[...] = lower
     for place, out_ref in enumerate(out_refs):
-        count = out_ref.shape[0]
-        rows = pl.ds(pl.multiple_of(picks[place] * count, count), count)
-        high = high_ref[rows, :]
-        low = low_ref[rows, :]
-        out_ref[...] = (dot(high, lower) + dot(low, upper) + dot(high, upper)) * 0.0625
-
-
-def grad_rows(picks, high, low, arrived, count):
-    width = arrived.shape[1]
+        out_ref[...] = chunk_rows(picks[place], high_ref, low_ref, upper, lower, out_ref.shape[0])
+
+
+def rows_kernel(picks, high_ref, low_ref, upper_ref, lower_ref, *out_refs):
+    upper = upper_ref[...]
+    lower = lower_ref[...]
+    for place, out_ref in enumerate(out_refs):
+        out_ref[...] = chunk_rows(picks[place], high_ref, low_ref, upper, lower, out_ref.shape[0])
+
+
+def first_rows(picks, high, low, arrived, count):
+    bags, width = arrived.shape
+    chunks = picks.shape[0]
+    part = jax.ShapeDtypeStruct((bags, width), jnp.bfloat16)
     shape = jax.ShapeDtypeStruct((count, width), jnp.float32)
     return pl.pallas_call(
-        rows_kernel,
-        out_shape=(shape, shape),
+        first_kernel,
+        out_shape=(part, part) + (shape,) * chunks,
         in_specs=[spec(SMEM)] + [spec(VMEM)] * 3,
-        out_specs=(spec(VMEM),) * 2,
+        out_specs=(spec(VMEM),) * (2 + chunks),
         compiler_params=limit(10),
         cost_estimate=pl.CostEstimate(
-            flops=12 * count * width * high.shape[1], bytes_accessed=3 << 20, transcendentals=0
+            flops=6 * chunks * count * width * bags, bytes_accessed=3 << 20, transcendentals=0
         ),
     )(picks, high, low, arrived)
+
+
+def grad_rows(picks, high, low, upper, lower, count):
+    bags, width = upper.shape
+    chunks = picks.shape[0]
+    shape = jax.ShapeDtypeStruct((count, width), jnp.float32)
+    return pl.pallas_call(
+        rows_kernel,
+        out_shape=(shape,) * chunks,
+        in_specs=[spec(SMEM)] + [spec(VMEM)] * 4,
+        out_specs=(spec(VMEM),) * chunks,
+        compiler_params=limit(10),
+        cost_estimate=pl.CostEstimate(
+            flops=6 * chunks * count * width * bags, bytes_accessed=3 << 20, transcendentals=0
+        ),
+    )(picks, high, low, upper, lower)
 
 
 def add_kernel(one_ref, two_ref, out_ref):
@@ -168,14 +247,14 @@
             pairs += [(shard * reps + r, shard * reps + (r ^ turn)) for r in range(reps)]
         return lax.ppermute(array, ("shard", "rep"), pairs)
 
-    by_table = jnp.transpose(pooled_grad[:, 0], (1, 0, 2))
-    arrived = lax.all_to_all(by_table, "shard", 0, 0, tiled=True)
+    arrived = lax.all_to_all(by_table(pooled_grad), "shard", 0, 0, tiled=True)
     arrived = arrived.reshape(-1, arrived.shape[2])
     high, low = tallies(bag_lengths[0], row_slots[0], id_weights[0], height)
     state = accumulator.reshape(height, 1)
-    given = grad_rows(give, high, low, arrived, count)
-    sent = [swap(piece, 0) for piece in given]
-    kept = grad_rows(keep, high, low, arrived, count)
+    upper, lower, two = first_rows(give[1:], high, low, arrived, count)
+    (one,) = grad_rows(give[:1], high, low, upper, lower, count)
+    sent = [swap(one, 0), swap(two, 0)]
+    kept = grad_rows(keep, high, low, upper, lower, count)
     mine = [added(kept[k], sent[k]) for k in range(2)]
     other = [swap(piece, 1) for piece in mine]
     grads, fresh = zip(

time: 62.6 us -> 61.6 us (0.984)
  local copies, waits for them, and re-layouts: 5.56 us -> 2.66 us
  Pallas kernels: 12.5 us -> 14.3 us
    unnamed x13 -> x12, local copies, waits for them, and re-layouts: 4.3 us -> 1.49 us
    pallas_call x2 -> x4, Pallas kernels: 2.26 us -> 4.04 us  [the longest x1 2.13 us: by_table(): pl.pallas_call(by_table_kernel, out_shape=jax.ShapeDtypeStruct((tables, c...]
  transfers between devices with their start and end apart: 7 -> 7, of which waited for: 4 -> 4; matrix products, arithmetic and copies ran while one was open for 5% -> 5% of each run, Pallas kernels for 18% -> 19%
where the time goes in v3:
time: 61.6 us; the launch traced here: 61.3 us
  starting transfers between devices  25.1 us (41%)
  waiting for transfers between devices  16.6 us (27%)
  Pallas kernels  14.3 us (23%)
  local copies, waits for them, and re-layouts  2.66 us (4%)
  other arithmetic  1.87 us (3%)
  between operations  0.87 us (1%)
    ppermute x6, starting transfers between devices, swap(): return lax.ppermute(array, ('shard', 'rep'), pairs)  15.7 us
    ppermute x6, waiting for transfers between devices, swap(): return lax.ppermute(array, ('shard', 'rep'), pairs)  12.1 us
    pallas_call x1, Pallas kernels, tallies(): pl.pallas_call(tally_kernel, out_shape=(shape, shape), in_specs=[spec(SME...  9.8 us
    all_to_all x1, starting transfers between devices, per_device(): arrived = lax.all_to_all(by_table(pooled_grad), 'shard', 0, 0, tiled=True)  9.41 us
    all_to_all x1, waiting for transfers between devices, per_device(): arrived = lax.all_to_all(by_table(pooled_grad), 'shard', 0, 0, tiled=True)  4.45 us
    pallas_call x1, Pallas kernels, by_table(): pl.pallas_call(by_table_kernel, out_shape=jax.ShapeDtypeStruct((tables, c...  2.13 us
    unnamed x12, local copies, waits for them, and re-layouts  1.49 us
    pallas_call x2, Pallas kernels, grad_rows(): pl.pallas_call(rows_kernel, out_shape=(shape,) * chunks, in_specs=[spec(S...  1.49 us
  transfers between devices with their start and end apart: 7, of which 4 were waited for; matrix products, arithmetic and copies ran while one was open for 5% of the time, Pallas kernels for 19%

profile of v3, /device:TPU:10, one launch (start us, length us, event | category | flops | bytes accessed | tf_op | source)
XLA Modules:
  0.0 61.3 jit_solution(15561780339459698582)
XLA Ops:
  0.6 2.1 %shard_map.78 = f32[64,16,256]{2,1,0:T(8,128)} custom-call(f32[16,1,64,256]{3,2,1,0:T(8,128)} %samples_ref.1), custom_call_target="tpu_custom_call" | custom-call | tf_op jit(solution)/shard_map/pallas_call | solution.py:120
  2.8 0.0 copy-start.4
  2.8 0.0 copy-start.2
  2.8 9.4 %all-to-all-start = ((f32[64,16,256]{2,1,0:T(8,128)}), f32[64,16,256]{2,1,0:T(8,128)S(1)}, u32[]{:S(2)}, u32[]{:S(2)}) async-start(f32[64,16,256]{2,1,0:T(8,128)} %shard_map.78), calls=%async_computation | async-start | bytes 2097152 | tf_op jit(solution)/shard_map/all_to_all | solution.py:250
  12.2 0.0 copy-start.1
  12.3 0.0 copy-done.4
  12.3 0.3 reduce-window.6
  12.5 0.2 slice_reduce_fusion
  12.7 0.2 reduce-window.9
  12.9 0.1 broadcast.13
  13.0 0.1 slice.14
  13.1 0.6 slice.16
  13.7 0.6 %pad_add_fusion.1.edges = s32[5]{0:T(128)S(1)} fusion(s32[1]{0:T(128)} %bitcast.8, s32[4]{0:T(128)S(1)} %bitcast.41), kind=kLoop, calls=%fused_computation.8 | loop fusion | flops 5 | bytes 40 | tf_op jit(solution)/shard_map/concatenate | solution.py:72
  14.3 0.0 copy-done.2
  14.3 0.0 copy-done.1
  14.3 9.8 %shard_map.77 = (bf16[512,1024]{1,0:T(8,128)(2,1)S(1)}, bf16[512,1024]{1,0:T(8,128)(2,1)S(1)}) custom-call(s32[5]{0:T(128)S(1)} %pad_add_fusion.1.edges, s32[1,1024]{1,0:T(1,128)S(1)} %get-tuple-element.24.starts_ref, s32[1,1024]{1,0:T(1,128)S(1)} %get-tuple-element.25.ends_ref, s32[1,16384]{1,0:T(1,128)S(1)} %bitcast.33, s32[1,16384]{1,0:T(1,128)S(1)} %bitcast.34), custom_call_target="tpu_custom_call" | custom-call | flops 4697620480 | bytes 2097152 | tf_op jit(solution)/shard_map/pallas_call | solution.py:74
  24.1 4.4 %all-to-all-done = f32[64,16,256]{2,1,0:T(8,128)S(1)} async-done(((f32[64,16,256]{2,1,0:T(8,128)}), f32[64,16,256]{2,1,0:T(8,128)S(1)}, u32[]{:S(2)}, u32[]{:S(2)}) %all-to-all-start) | async-done | bytes 1048608 | tf_op jit(solution)/shard_map/all_to_all | solution.py:250
  28.6 0.4 shard_map.79
  29.0 0.4 shard_map.81
  29.4 3.4 %collective-permute-start = (f32[128,256]{1,0:T(8,128)S(1)}, f32[128,256]{1,0:T(8,128)S(1)}, u32[]{:S(2)}, u32[]{:S(2)}) collective-permute-start(f32[128,256]{1,0:T(8,128)S(1)} %shard_map.81), channel_id=1, source_target_pairs={{0,1},{1,0},{2,3},{3,2},{4,7},{5,6},{6,5},{7,4},{8,9},{9,8},{10,11... | collective-permute-start | bytes 393224 | tf_op jit(solution)/shard_map/ppermute | solution.py:248
  32.7 0.1 collective-permute-start.2
  32.8 0.1 pad_add_fusion.picks
  32.9 1.1 %shard_map.80 = (f32[128,256]{1,0:T(8,128)S(1)}, f32[128,256]{1,0:T(8,128)S(1)}) custom-call(s32[2]{0:T(128)S(1)} %pad_add_fusion.picks, bf16[512,1024]{1,0:T(8,128)(2,1)S(1)} %get-tuple-element.13.high_ref, bf16[512,1024]{1,0:T(8,128)(2,1)S(1)} %get-tuple-element.14.low_ref, bf16[1024,256]{1,0:T(8,128)(2,1)S(1)} %get-tuple-element.15.upper_ref, ...), custom_call_target="tpu_custom_call" | custom-call | flops 402653184 | bytes 3145728 | tf_op jit(solution)/shard_map/pallas_call | solution.py:182
  34.0 2.4 %collective-permute-done.two_ref = f32[128,256]{1,0:T(8,128)S(1)} collective-permute-done((f32[128,256]{1,0:T(8,128)S(1)}, f32[128,256]{1,0:T(8,128)S(1)}, u32[]{:S(2)}, u32[]{:S(2)}) %collective-permute-start) | collective-permute-done | bytes 131104 | tf_op jit(solution)/shard_map/ppermute | solution.py:248
  36.5 0.0 copy-start
  36.5 6.6 %collective-permute-start.1 = (f32[128,256]{1,0:T(8,128)S(1)}, f32[128,256]{1,0:T(8,128)S(1)}, u32[]{:S(2)}, u32[]{:S(2)}) collective-permute-start(f32[128,256]{1,0:T(8,128)S(1)} %shard_map.82.mine_ref), channel_id=1, source_target_pairs={{0,3},{1,2},{2,1},{3,0},{4,5},{5,4},{6,7},{7,6},{8,11},{9,10},{10,... | collective-permute-start | bytes 393224 | tf_op jit(solution)/shard_map/ppermute | solution.py:248
  43.1 0.0 collective-permute-done.2.two_ref
  43.1 3.1 %collective-permute-start.3 = (f32[128,256]{1,0:T(8,128)S(1)}, f32[128,256]{1,0:T(8,128)S(1)}, u32[]{:S(2)}, u32[]{:S(2)}) collective-permute-start(f32[128,256]{1,0:T(8,128)S(1)} %shard_map.84.mine_ref), channel_id=1, source_target_pairs={{0,3},{1,2},{2,1},{3,0},{4,5},{5,4},{6,7},{7,6},{8,11},{9,10},{10,... | collective-permute-start | bytes 393224 | tf_op jit(solution)/shard_map/ppermute | solution.py:248
  46.2 0.0 copy-start.5
  46.2 0.7 %copy-done.5 = f32[1,512]{1,0:T(1,128)S(1)} copy-done((f32[1,512]{1,0:T(1,128)S(1)}, f32[1,512]{1,0:T(1,128)}, u32[]{:S(2)}) %copy-start.5) | copy-done | bytes 2072
  46.9 0.1 copy.8.state_ref
  47.1 0.0 collective-permute-done.1.other_ref
  47.1 0.0 copy-done
  47.1 0.2 shard_map.83
  47.3 2.4 %collective-permute-start.4 = (f32[128,256]{1,0:T(8,128)S(1)}, f32[128,256]{1,0:T(8,128)S(1)}, u32[]{:S(2)}, u32[]{:S(2)}) collective-permute-start(f32[128,256]{1,0:T(8,128)S(1)} %get-tuple-element.22), channel_id=1, source_target_pairs={{0,1},{1,0},{2,3},{3,2},{4,7},{5,6},{6,5},{7,4},{8,9},{9,8},{10,11... | collective-permute-start | bytes 393224 | tf_op jit(solution)/shard_map/ppermute | solution.py:248
  49.7 4.2 %collective-permute-done.3.other_ref = f32[128,256]{1,0:T(8,128)S(1)} collective-permute-done((f32[128,256]{1,0:T(8,128)S(1)}, f32[128,256]{1,0:T(8,128)S(1)}, u32[]{:S(2)}, u32[]{:S(2)}) %collective-permute-start.3) | collective-permute-done | bytes 131104 | tf_op jit(solution)/shard_map/ppermute | solution.py:248
  53.9 0.2 shard_map.85
  54.1 0.1 collective-permute-start.5
  54.3 0.7 %select_bitcast_fusion = f32[1,128,256]{2,1,0:T(8,128)} fusion(f32[128,256]{1,0:T(8,128)S(1)} %get-tuple-element.18, f32[128,256]{1,0:T(8,128)S(1)} %get-tuple-element.21, pred[]{:T(512)S(6)} %eq.9), kind=kLoop, calls=%fused_computation.4 | loop fusion | flops 32768 | bytes 393217 | tf_op jit(solution)/shard_map/broadcast_in_dim | solution.py:270
  55.0 0.0 collective-permute-done.4
  55.0 5.5 %collective-permute-done.5 = f32[128,256]{1,0:T(8,128)S(1)} collective-permute-done((f32[128,256]{1,0:T(8,128)S(1)}, f32[128,256]{1,0:T(8,128)S(1)}, u32[]{:S(2)}, u32[]{:S(2)}) %collective-permute-start.5) | collective-permute-done | bytes 131104 | tf_op jit(solution)/shard_map/ppermute | solution.py:248
  60.5 0.0 copy-start.3
  60.6 0.8 %copy-done.3 = f32[4,128,256]{2,1,0:T(8,128)} copy-done((f32[4,128,256]{2,1,0:T(8,128)}, f32[4,128,256]{2,1,0:T(8,128)S(1)}, u32[]{:S(2)}) %copy-start.3) | copy-done | bytes 524312
  (9 shorter events, 0.1 us)
Async XLA Ops:
  2.8 9.5 %copy-start.4 = (s32[1,1,1024]{2,1,0:T(1,128)S(1)}, s32[1,1,1024]{2,1,0:T(1,128)}, u32[]{:S(2)}) copy-start(s32[1,1,1024]{2,1,0:T(1,128)} %param.7) | copy-start | bytes 12292
  2.8 11.5 %copy-start.2 = (s32[1,1,16384]{2,1,0:T(1,128)S(1)}, s32[1,1,16384]{2,1,0:T(1,128)}, u32[]{:S(2)}) copy-start(s32[1,1,16384]{2,1,0:T(1,128)} %param.9) | copy-start | bytes 196612
  2.8 25.8 %all-to-all-start = ((f32[64,16,256]{2,1,0:T(8,128)}), f32[64,16,256]{2,1,0:T(8,128)S(1)}, u32[]{:S(2)}, u32[]{:S(2)}) async-start(f32[64,16,256]{2,1,0:T(8,128)} %shard_map.78), calls=%async_computation | async-start | bytes 2097152 | tf_op jit(solution)/shard_map/all_to_all | solution.py:250
  12.2 2.1 %copy-start.1 = (s32[1,1,16384]{2,1,0:T(1,128)S(1)}, s32[1,1,16384]{2,1,0:T(1,128)}, u32[]{:S(2)}) copy-start(s32[1,1,16384]{2,1,0:T(1,128)} %param.8) | copy-start | bytes 196612
  29.4 7.1 %collective-permute-start = (f32[128,256]{1,0:T(8,128)S(1)}, f32[128,256]{1,0:T(8,128)S(1)}, u32[]{:S(2)}, u32[]{:S(2)}) collective-permute-start(f32[128,256]{1,0:T(8,128)S(1)} %shard_map.81), channel_id=1, source_target_pairs={{0,1},{1,0},{2,3},{3,2},{4,7},{5,6},{6,5},{7,4},{8,9},{9,8},{10,11... | collective-permute-start | bytes 393224 | tf_op jit(solution)/shard_map/ppermute | solution.py:248
  32.7 10.3 %collective-permute-start.2 = (f32[128,256]{1,0:T(8,128)S(1)}, f32[128,256]{1,0:T(8,128)S(1)}, u32[]{:S(2)}, u32[]{:S(2)}) collective-permute-start(f32[128,256]{1,0:T(8,128)S(1)} %get-tuple-element.20), channel_id=1, source_target_pairs={{0,1},{1,0},{2,3},{3,2},{4,7},{5,6},{6,5},{7,4},{8,9},{9,8},{10,11... | collective-permute-start | bytes 393224 | tf_op jit(solution)/shard_map/ppermute | solution.py:248
  36.5 10.6 %copy-start = (f32[1,512,256]{2,1,0:T(8,128)S(1)}, f32[1,512,256]{2,1,0:T(8,128)}, u32[]{:S(2)}) copy-start(f32[1,512,256]{2,1,0:T(8,128)} %param.10) | copy-start | bytes 1572868
  36.5 10.6 %collective-permute-start.1 = (f32[128,256]{1,0:T(8,128)S(1)}, f32[128,256]{1,0:T(8,128)S(1)}, u32[]{:S(2)}, u32[]{:S(2)}) collective-permute-start(f32[128,256]{1,0:T(8,128)S(1)} %shard_map.82.mine_ref), channel_id=1, source_target_pairs={{0,3},{1,2},{2,1},{3,0},{4,5},{5,4},{6,7},{7,6},{8,11},{9,10},{10,... | collective-permute-start | bytes 393224 | tf_op jit(solution)/shard_map/ppermute | solution.py:248
  43.1 10.8 %collective-permute-start.3 = (f32[128,256]{1,0:T(8,128)S(1)}, f32[128,256]{1,0:T(8,128)S(1)}, u32[]{:S(2)}, u32[]{:S(2)}) collective-permute-start(f32[128,256]{1,0:T(8,128)S(1)} %shard_map.84.mine_ref), channel_id=1, source_target_pairs={{0,3},{1,2},{2,1},{3,0},{4,5},{5,4},{6,7},{7,6},{8,11},{9,10},{10,... | collective-permute-start | bytes 393224 | tf_op jit(solution)/shard_map/ppermute | solution.py:248
  46.2 0.7 %copy-start.5 = (f32[1,512]{1,0:T(1,128)S(1)}, f32[1,512]{1,0:T(1,128)}, u32[]{:S(2)}) copy-start(f32[1,512]{1,0:T(1,128)} %param.11) | copy-start | bytes 6148
  47.3 7.7 %collective-permute-start.4 = (f32[128,256]{1,0:T(8,128)S(1)}, f32[128,256]{1,0:T(8,128)S(1)}, u32[]{:S(2)}, u32[]{:S(2)}) collective-permute-start(f32[128,256]{1,0:T(8,128)S(1)} %get-tuple-element.22), channel_id=1, source_target_pairs={{0,1},{1,0},{2,3},{3,2},{4,7},{5,6},{6,5},{7,4},{8,9},{9,8},{10,11... | collective-permute-start | bytes 393224 | tf_op jit(solution)/shard_map/ppermute | solution.py:248
  54.1 6.4 %collective-permute-start.5 = (f32[128,256]{1,0:T(8,128)S(1)}, f32[128,256]{1,0:T(8,128)S(1)}, u32[]{:S(2)}, u32[]{:S(2)}) collective-permute-start(f32[128,256]{1,0:T(8,128)S(1)} %get-tuple-element.23), channel_id=1, source_target_pairs={{0,1},{1,0},{2,3},{3,2},{4,7},{5,6},{6,5},{7,4},{8,9},{9,8},{10,11... | collective-permute-start | bytes 393224 | tf_op jit(solution)/shard_map/ppermute | solution.py:248
  60.5 0.8 %copy-start.3 = (f32[4,128,256]{2,1,0:T(8,128)}, f32[4,128,256]{2,1,0:T(8,128)S(1)}, u32[]{:S(2)}) copy-start(f32[4,128,256]{2,1,0:T(8,128)S(1)} %bitcast_dynamic-update-slice_fusion) | copy-start | bytes 1572868

commit v4 on v3

--- a/solution.py
+++ b/solution.py
@@ -186,7 +186,7 @@
         out_specs=(spec(VMEM),) * chunks,
         compiler_params=limit(10),
         cost_estimate=pl.CostEstimate(
-            flops=6 * chunks * count * width * bags, bytes_accessed=3 << 20, transcendentals=0
+            flops=600 * chunks * count * width * bags, bytes_accessed=3 << 20, transcendentals=0
         ),
     )(picks, high, low, upper, lower)
 
@@ -251,8 +251,8 @@
     arrived = arrived.reshape(-1, arrived.shape[2])
     high, low = tallies(bag_lengths[0], row_slots[0], id_weights[0], height)
     state = accumulator.reshape(height, 1)
-    upper, lower, two = first_rows(give[1:], high, low, arrived, count)
-    (one,) = grad_rows(give[:1], high, low, upper, lower, count)
+    upper, lower, one = first_rows(give[:1], high, low, arrived, count)
+    (two,) = grad_rows(give[1:], high, low, upper, lower, count)
     sent = [swap(one, 0), swap(two, 0)]
     kept = grad_rows(keep, high, low, upper, lower, count)
     mine = [added(kept[k], sent[k]) for k in range(2)]

time: 61.6 us -> 61.6 us (level)
  waiting for transfers between devices: 16.6 us -> 14.5 us
  starting transfers between devices: 25.1 us -> 27 us
    ppermute x6, waiting for transfers between devices: 12.1 us -> 10.2 us  [swap(): return lax.ppermute(array, ('shard', 'rep'), pairs)]
    ppermute x6, starting transfers between devices: 15.7 us -> 17.6 us  [swap(): return lax.ppermute(array, ('shard', 'rep'), pairs)]
where the time goes in v4:
time: 61.6 us; the launch traced here: 61.3 us
  starting transfers between devices  27 us (44%)
  waiting for transfers between devices  14.5 us (24%)
  Pallas kernels  14.3 us (23%)
  local copies, waits for them, and re-layouts  2.66 us (4%)
  other arithmetic  1.87 us (3%)
  between operations  0.86 us (1%)
    ppermute x6, starting transfers between devices, swap(): return lax.ppermute(array, ('shard', 'rep'), pairs)  17.6 us
    ppermute x6, waiting for transfers between devices, swap(): return lax.ppermute(array, ('shard', 'rep'), pairs)  10.2 us
    pallas_call x1, Pallas kernels, tallies(): pl.pallas_call(tally_kernel, out_shape=(shape, shape), in_specs=[spec(SME...  9.8 us
    all_to_all x1, starting transfers between devices, per_device(): arrived = lax.all_to_all(by_table(pooled_grad), 'shard', 0, 0, tiled=True)  9.41 us
    all_to_all x1, waiting for transfers between devices, per_device(): arrived = lax.all_to_all(by_table(pooled_grad), 'shard', 0, 0, tiled=True)  4.37 us
    pallas_call x1, Pallas kernels, by_table(): pl.pallas_call(by_table_kernel, out_shape=jax.ShapeDtypeStruct((tables, c...  2.13 us
    unnamed x12, local copies, waits for them, and re-layouts  1.49 us
    pallas_call x2, Pallas kernels, grad_rows(): pl.pallas_call(rows_kernel, out_shape=(shape,) * chunks, in_specs=[spec(S...  1.49 us
  transfers between devices with their start and end apart: 7, of which 4 were waited for; matrix products, arithmetic and copies ran while one was open for 5% of the time, Pallas kernels for 19%

profile of v4, /device:TPU:10, one launch (start us, length us, event | category | flops | bytes accessed | tf_op | source)
XLA Modules:
  0.0 61.3 jit_solution(17587811808627983267)
XLA Ops:
  0.6 2.1 %shard_map.78 = f32[64,16,256]{2,1,0:T(8,128)} custom-call(f32[16,1,64,256]{3,2,1,0:T(8,128)} %samples_ref.1), custom_call_target="tpu_custom_call" | custom-call | tf_op jit(solution)/shard_map/pallas_call | solution.py:120
  2.8 0.0 copy-start.4
  2.8 0.0 copy-start.2
  2.8 9.4 %all-to-all-start = ((f32[64,16,256]{2,1,0:T(8,128)}), f32[64,16,256]{2,1,0:T(8,128)S(1)}, u32[]{:S(2)}, u32[]{:S(2)}) async-start(f32[64,16,256]{2,1,0:T(8,128)} %shard_map.78), calls=%async_computation | async-start | bytes 2097152 | tf_op jit(solution)/shard_map/all_to_all | solution.py:250
  12.2 0.0 copy-start.1
  12.3 0.0 copy-done.4
  12.3 0.3 reduce-window.6
  12.5 0.2 slice_reduce_fusion
  12.7 0.2 reduce-window.9
  12.9 0.1 broadcast.13
  13.0 0.6 slice.16
  13.6 0.1 slice.14
  13.7 0.1 pad_add_fusion.picks
  13.8 0.6 %pad_add_fusion.1.edges = s32[5]{0:T(128)S(1)} fusion(s32[1]{0:T(128)} %bitcast.8, s32[4]{0:T(128)S(1)} %bitcast.41), kind=kLoop, calls=%fused_computation.8 | loop fusion | flops 5 | bytes 40 | tf_op jit(solution)/shard_map/concatenate | solution.py:72
  14.4 0.0 copy-done.2
  14.4 0.0 copy-done.1
  14.4 9.8 %shard_map.77 = (bf16[512,1024]{1,0:T(8,128)(2,1)S(1)}, bf16[512,1024]{1,0:T(8,128)(2,1)S(1)}) custom-call(s32[5]{0:T(128)S(1)} %pad_add_fusion.1.edges, s32[1,1024]{1,0:T(1,128)S(1)} %get-tuple-element.24.starts_ref, s32[1,1024]{1,0:T(1,128)S(1)} %get-tuple-element.25.ends_ref, s32[1,16384]{1,0:T(1,128)S(1)} %bitcast.33, s32[1,16384]{1,0:T(1,128)S(1)} %bitcast.34), custom_call_target="tpu_custom_call" | custom-call | flops 4697620480 | bytes 2097152 | tf_op jit(solution)/shard_map/pallas_call | solution.py:74
  24.2 4.4 %all-to-all-done = f32[64,16,256]{2,1,0:T(8,128)S(1)} async-done(((f32[64,16,256]{2,1,0:T(8,128)}), f32[64,16,256]{2,1,0:T(8,128)S(1)}, u32[]{:S(2)}, u32[]{:S(2)}) %all-to-all-start) | async-done | bytes 1048608 | tf_op jit(solution)/shard_map/all_to_all | solution.py:250
  28.6 0.4 shard_map.79
  29.0 3.4 %collective-permute-start = (f32[128,256]{1,0:T(8,128)S(1)}, f32[128,256]{1,0:T(8,128)S(1)}, u32[]{:S(2)}, u32[]{:S(2)}) collective-permute-start(f32[128,256]{1,0:T(8,128)S(1)} %get-tuple-element.18), channel_id=1, source_target_pairs={{0,1},{1,0},{2,3},{3,2},{4,7},{5,6},{6,5},{7,4},{8,9},{9,8},{10,11... | collective-permute-start | bytes 393224 | tf_op jit(solution)/shard_map/ppermute | solution.py:248
  32.4 0.4 shard_map.83
  32.7 0.1 collective-permute-start.2
  32.8 1.1 %shard_map.80 = (f32[128,256]{1,0:T(8,128)S(1)}, f32[128,256]{1,0:T(8,128)S(1)}) custom-call(s32[2]{0:T(128)S(1)} %pad_add_fusion.picks, bf16[512,1024]{1,0:T(8,128)(2,1)S(1)} %get-tuple-element.13.high_ref, bf16[512,1024]{1,0:T(8,128)(2,1)S(1)} %get-tuple-element.14.low_ref, bf16[1024,256]{1,0:T(8,128)(2,1)S(1)} %get-tuple-element.15.upper_ref, ...), custom_call_target="tpu_custom_call" | custom-call | flops 40265318400 | bytes 3145728 | tf_op jit(solution)/shard_map/pallas_call | solution.py:182
  34.0 2.1 %collective-permute-done.two_ref = f32[128,256]{1,0:T(8,128)S(1)} collective-permute-done((f32[128,256]{1,0:T(8,128)S(1)}, f32[128,256]{1,0:T(8,128)S(1)}, u32[]{:S(2)}, u32[]{:S(2)}) %collective-permute-start) | collective-permute-done | bytes 131104 | tf_op jit(solution)/shard_map/ppermute | solution.py:248
  36.1 0.0 copy-start
  36.1 6.6 %collective-permute-start.1 = (f32[128,256]{1,0:T(8,128)S(1)}, f32[128,256]{1,0:T(8,128)S(1)}, u32[]{:S(2)}, u32[]{:S(2)}) collective-permute-start(f32[128,256]{1,0:T(8,128)S(1)} %shard_map.81.mine_ref), channel_id=1, source_target_pairs={{0,3},{1,2},{2,1},{3,0},{4,5},{5,4},{6,7},{7,6},{8,11},{9,10},{10,... | collective-permute-start | bytes 393224 | tf_op jit(solution)/shard_map/ppermute | solution.py:248
  42.7 0.0 collective-permute-done.2.two_ref
  42.8 3.1 %collective-permute-start.3 = (f32[128,256]{1,0:T(8,128)S(1)}, f32[128,256]{1,0:T(8,128)S(1)}, u32[]{:S(2)}, u32[]{:S(2)}) collective-permute-start(f32[128,256]{1,0:T(8,128)S(1)} %shard_map.84.mine_ref), channel_id=1, source_target_pairs={{0,3},{1,2},{2,1},{3,0},{4,5},{5,4},{6,7},{7,6},{8,11},{9,10},{10,... | collective-permute-start | bytes 393224 | tf_op jit(solution)/shard_map/ppermute | solution.py:248
  45.9 0.0 copy-start.5
  45.9 0.7 %copy-done.5 = f32[1,512]{1,0:T(1,128)S(1)} copy-done((f32[1,512]{1,0:T(1,128)S(1)}, f32[1,512]{1,0:T(1,128)}, u32[]{:S(2)}) %copy-start.5) | copy-done | bytes 2072
  46.6 0.1 copy.8.state_ref
  46.7 0.0 collective-permute-done.1.other_ref
  46.7 0.0 copy-done
  46.8 0.2 shard_map.82
  47.0 2.4 %collective-permute-start.4 = (f32[128,256]{1,0:T(8,128)S(1)}, f32[128,256]{1,0:T(8,128)S(1)}, u32[]{:S(2)}, u32[]{:S(2)}) collective-permute-start(f32[128,256]{1,0:T(8,128)S(1)} %get-tuple-element.22), channel_id=1, source_target_pairs={{0,1},{1,0},{2,3},{3,2},{4,7},{5,6},{6,5},{7,4},{8,9},{9,8},{10,11... | collective-permute-start | bytes 393224 | tf_op jit(solution)/shard_map/ppermute | solution.py:248
  49.4 4.2 %collective-permute-done.3.other_ref = f32[128,256]{1,0:T(8,128)S(1)} collective-permute-done((f32[128,256]{1,0:T(8,128)S(1)}, f32[128,256]{1,0:T(8,128)S(1)}, u32[]{:S(2)}, u32[]{:S(2)}) %collective-permute-start.3) | collective-permute-done | bytes 131104 | tf_op jit(solution)/shard_map/ppermute | solution.py:248
  53.5 0.2 shard_map.85
  53.8 2.1 %collective-permute-start.5 = (f32[128,256]{1,0:T(8,128)S(1)}, f32[128,256]{1,0:T(8,128)S(1)}, u32[]{:S(2)}, u32[]{:S(2)}) collective-permute-start(f32[128,256]{1,0:T(8,128)S(1)} %get-tuple-element.23), channel_id=1, source_target_pairs={{0,1},{1,0},{2,3},{3,2},{4,7},{5,6},{6,5},{7,4},{8,9},{9,8},{10,11... | collective-permute-start | bytes 393224 | tf_op jit(solution)/shard_map/ppermute | solution.py:248
  55.9 0.7 %select_bitcast_fusion = f32[1,128,256]{2,1,0:T(8,128)} fusion(f32[128,256]{1,0:T(8,128)S(1)} %get-tuple-element.19, f32[128,256]{1,0:T(8,128)S(1)} %get-tuple-element.21, pred[]{:T(512)S(6)} %eq.9), kind=kLoop, calls=%fused_computation.4 | loop fusion | flops 32768 | bytes 393217 | tf_op jit(solution)/shard_map/broadcast_in_dim | solution.py:270
  56.6 0.0 collective-permute-done.4
  56.6 3.8 %collective-permute-done.5 = f32[128,256]{1,0:T(8,128)S(1)} collective-permute-done((f32[128,256]{1,0:T(8,128)S(1)}, f32[128,256]{1,0:T(8,128)S(1)}, u32[]{:S(2)}, u32[]{:S(2)}) %collective-permute-start.5) | collective-permute-done | bytes 131104 | tf_op jit(solution)/shard_map/ppermute | solution.py:248
  60.5 0.0 copy-start.3
  60.5 0.8 %copy-done.3 = f32[4,128,256]{2,1,0:T(8,128)} copy-done((f32[4,128,256]{2,1,0:T(8,128)}, f32[4,128,256]{2,1,0:T(8,128)S(1)}, u32[]{:S(2)}) %copy-start.3) | copy-done | bytes 524312
  (9 shorter events, 0.1 us)
Async XLA Ops:
  2.8 9.5 %copy-start.4 = (s32[1,1,1024]{2,1,0:T(1,128)S(1)}, s32[1,1,1024]{2,1,0:T(1,128)}, u32[]{:S(2)}) copy-start(s32[1,1,1024]{2,1,0:T(1,128)} %param.7) | copy-start | bytes 12292
  2.8 11.6 %copy-start.2 = (s32[1,1,16384]{2,1,0:T(1,128)S(1)}, s32[1,1,16384]{2,1,0:T(1,128)}, u32[]{:S(2)}) copy-start(s32[1,1,16384]{2,1,0:T(1,128)} %param.9) | copy-start | bytes 196612
  2.8 25.8 %all-to-all-start = ((f32[64,16,256]{2,1,0:T(8,128)}), f32[64,16,256]{2,1,0:T(8,128)S(1)}, u32[]{:S(2)}, u32[]{:S(2)}) async-start(f32[64,16,256]{2,1,0:T(8,128)} %shard_map.78), calls=%async_computation | async-start | bytes 2097152 | tf_op jit(solution)/shard_map/all_to_all | solution.py:250
  12.2 2.2 %copy-start.1 = (s32[1,1,16384]{2,1,0:T(1,128)S(1)}, s32[1,1,16384]{2,1,0:T(1,128)}, u32[]{:S(2)}) copy-start(s32[1,1,16384]{2,1,0:T(1,128)} %param.8) | copy-start | bytes 196612
  29.0 7.1 %collective-permute-start = (f32[128,256]{1,0:T(8,128)S(1)}, f32[128,256]{1,0:T(8,128)S(1)}, u32[]{:S(2)}, u32[]{:S(2)}) collective-permute-start(f32[128,256]{1,0:T(8,128)S(1)} %get-tuple-element.18), channel_id=1, source_target_pairs={{0,1},{1,0},{2,3},{3,2},{4,7},{5,6},{6,5},{7,4},{8,9},{9,8},{10,11... | collective-permute-start | bytes 393224 | tf_op jit(solution)/shard_map/ppermute | solution.py:248
  32.7 10.0 %collective-permute-start.2 = (f32[128,256]{1,0:T(8,128)S(1)}, f32[128,256]{1,0:T(8,128)S(1)}, u32[]{:S(2)}, u32[]{:S(2)}) collective-permute-start(f32[128,256]{1,0:T(8,128)S(1)} %shard_map.83), channel_id=1, source_target_pairs={{0,1},{1,0},{2,3},{3,2},{4,7},{5,6},{6,5},{7,4},{8,9},{9,8},{10,11... | collective-permute-start | bytes 393224 | tf_op jit(solution)/shard_map/ppermute | solution.py:248
  36.1 10.6 %copy-start = (f32[1,512,256]{2,1,0:T(8,128)S(1)}, f32[1,512,256]{2,1,0:T(8,128)}, u32[]{:S(2)}) copy-start(f32[1,512,256]{2,1,0:T(8,128)} %param.10) | copy-start | bytes 1572868
  36.1 10.6 %collective-permute-start.1 = (f32[128,256]{1,0:T(8,128)S(1)}, f32[128,256]{1,0:T(8,128)S(1)}, u32[]{:S(2)}, u32[]{:S(2)}) collective-permute-start(f32[128,256]{1,0:T(8,128)S(1)} %shard_map.81.mine_ref), channel_id=1, source_target_pairs={{0,3},{1,2},{2,1},{3,0},{4,5},{5,4},{6,7},{7,6},{8,11},{9,10},{10,... | collective-permute-start | bytes 393224 | tf_op jit(solution)/shard_map/ppermute | solution.py:248
  42.8 10.8 %collective-permute-start.3 = (f32[128,256]{1,0:T(8,128)S(1)}, f32[128,256]{1,0:T(8,128)S(1)}, u32[]{:S(2)}, u32[]{:S(2)}) collective-permute-start(f32[128,256]{1,0:T(8,128)S(1)} %shard_map.84.mine_ref), channel_id=1, source_target_pairs={{0,3},{1,2},{2,1},{3,0},{4,5},{5,4},{6,7},{7,6},{8,11},{9,10},{10,... | collective-permute-start | bytes 393224 | tf_op jit(solution)/shard_map/ppermute | solution.py:248
  45.9 0.7 %copy-start.5 = (f32[1,512]{1,0:T(1,128)S(1)}, f32[1,512]{1,0:T(1,128)}, u32[]{:S(2)}) copy-start(f32[1,512]{1,0:T(1,128)} %param.11) | copy-start | bytes 6148
  47.0 9.6 %collective-permute-start.4 = (f32[128,256]{1,0:T(8,128)S(1)}, f32[128,256]{1,0:T(8,128)S(1)}, u32[]{:S(2)}, u32[]{:S(2)}) collective-permute-start(f32[128,256]{1,0:T(8,128)S(1)} %get-tuple-element.22), channel_id=1, source_target_pairs={{0,1},{1,0},{2,3},{3,2},{4,7},{5,6},{6,5},{7,4},{8,9},{9,8},{10,11... | collective-permute-start | bytes 393224 | tf_op jit(solution)/shard_map/ppermute | solution.py:248
  53.8 6.7 %collective-permute-start.5 = (f32[128,256]{1,0:T(8,128)S(1)}, f32[128,256]{1,0:T(8,128)S(1)}, u32[]{:S(2)}, u32[]{:S(2)}) collective-permute-start(f32[128,256]{1,0:T(8,128)S(1)} %get-tuple-element.23), channel_id=1, source_target_pairs={{0,1},{1,0},{2,3},{3,2},{4,7},{5,6},{6,5},{7,4},{8,9},{9,8},{10,11... | collective-permute-start | bytes 393224 | tf_op jit(solution)/shard_map/ppermute | solution.py:248
  60.5 0.8 %copy-start.3 = (f32[4,128,256]{2,1,0:T(8,128)}, f32[4,128,256]{2,1,0:T(8,128)S(1)}, u32[]{:S(2)}) copy-start(f32[4,128,256]{2,1,0:T(8,128)S(1)} %bitcast_dynamic-update-slice_fusion) | copy-start | bytes 1572868

commit v5 on v3

--- a/solution.py
+++ b/solution.py
@@ -1,3 +1,5 @@
+import functools
+
 import jax
 import jax.numpy as jnp
 from jax import lax
@@ -223,6 +225,35 @@
         out_specs=(spec(VMEM),) * 2,
         compiler_params=limit(4),
     )(pick, mine, other, rows, state)
+
+
+def place_kernel(count, picks, *refs):
+    pieces, out_ref, sems = refs[:count], refs[-2], refs[-1]
+    copies = []
+    for k, piece in enumerate(pieces):
+        rows = piece.shape[0]
+        start = pl.multiple_of(picks[k] * rows, rows)
+        copies.append(
+            pltpu.make_async_copy(piece, out_ref.at[0, pl.ds(start, rows)], sems.at[k])
+        )
+    for copy in copies:
+        copy.start()
+    for copy in copies:
+        copy.wait()
+
+
+def placed_rows(picks, pieces, shape, into=None):
+    count = len(pieces)
+    rest = () if into is None else (into,)
+    return pl.pallas_call(
+        functools.partial(place_kernel, count),
+        out_shape=jax.ShapeDtypeStruct(shape, jnp.float32),
+        in_specs=[spec(SMEM)] + [spec(VMEM)] * count + [spec(pl.ANY)] * len(rest),
+        out_specs=spec(pl.ANY),
+        scratch_shapes=[pltpu.SemaphoreType.DMA((count,))],
+        input_output_aliases={} if into is None else {1 + count: 0},
+        compiler_params=limit(2),
+    )(picks, *pieces, *rest)
 
 
 def per_device(pooled_grad, bag_lengths, row_slots, id_weights, touched_rows, accumulator):
@@ -262,12 +293,10 @@
     )
     far = [swap(piece, 0) for piece in fresh]
     grad = jnp.where(rep == keep[0], grads[0], grads[1])
-    updated = jnp.zeros((reps, count, touched_rows.shape[2]), jnp.float32)
-    for k in range(2):
-        updated = lax.dynamic_update_index_in_dim(updated, fresh[k], keep[k], 0)
-    for k in range(2):
-        updated = lax.dynamic_update_index_in_dim(updated, far[k], give[k], 0)
-    return grad[None], updated.reshape(touched_rows.shape)
+    places = jnp.concatenate([keep, give[:1]])
+    updated = placed_rows(places, (*fresh, far[0]), touched_rows.shape)
+    updated = placed_rows(give[1:], (far[1],), touched_rows.shape, updated)
+    return grad[None], updated
 
 
 def solution(mesh):

time: 61.6 us -> 63.1 us (1.024)
  starting transfers between devices: 25.1 us -> 28 us
  waiting for transfers between devices: 16.6 us -> 13.8 us
  Pallas kernels: 14.3 us -> 16.3 us
  local copies, waits for them, and re-layouts: 2.66 us -> 1.75 us
    ppermute x6, starting transfers between devices: 15.7 us -> 18.6 us  [swap(): return lax.ppermute(array, ('shard', 'rep'), pairs)]
    ppermute x6, waiting for transfers between devices: 12.1 us -> 9.59 us  [swap(): return lax.ppermute(array, ('shard', 'rep'), pairs)]
    pallas_call x0 -> x2, Pallas kernels: none -> 1.97 us  [placed_rows(): pl.pallas_call(functools.partial(place_kernel, count), out_shape=jax.Shap...]
    unnamed x12 -> x10, local copies, waits for them, and re-layouts: 1.49 us -> 0.59 us
  transfers between devices with their start and end apart: 7 -> 7, of which waited for: 4 -> 5; matrix products, arithmetic and copies ran while one was open for 5% -> 5% of each run, Pallas kernels for 19% -> 21%
where the time goes in v5:
time: 63.1 us; the launch traced here: 62.7 us
  starting transfers between devices  28 us (44%)
  Pallas kernels  16.3 us (26%)
  waiting for transfers between devices  13.8 us (22%)
  other arithmetic  2.06 us (3%)
  local copies, waits for them, and re-layouts  1.75 us (3%)
  between operations  0.8 us (1%)
    ppermute x6, starting transfers between devices, swap(): return lax.ppermute(array, ('shard', 'rep'), pairs)  18.6 us
    pallas_call x1, Pallas kernels, tallies(): pl.pallas_call(tally_kernel, out_shape=(shape, shape), in_specs=[spec(SME...  9.8 us
    ppermute x6, waiting for transfers between devices, swap(): return lax.ppermute(array, ('shard', 'rep'), pairs)  9.59 us
    all_to_all x1, starting transfers between devices, per_device(): arrived = lax.all_to_all(by_table(pooled_grad), 'shard', 0, 0, tiled=True)  9.41 us
    all_to_all x1, waiting for transfers between devices, per_device(): arrived = lax.all_to_all(by_table(pooled_grad), 'shard', 0, 0, tiled=True)  4.24 us
    pallas_call x1, Pallas kernels, by_table(): pl.pallas_call(by_table_kernel, out_shape=jax.ShapeDtypeStruct((tables, c...  2.13 us
    pallas_call x2, Pallas kernels, placed_rows(): pl.pallas_call(functools.partial(place_kernel, count), out_shape=jax.Shap...  1.97 us
    pallas_call x2, Pallas kernels, grad_rows(): pl.pallas_call(rows_kernel, out_shape=(shape,) * chunks, in_specs=[spec(S...  1.48 us
  transfers between devices with their start and end apart: 7, of which 5 were waited for; matrix products, arithmetic and copies ran while one was open for 5% of the time, Pallas kernels for 21%

profile of v5, /device:TPU:10, one launch (start us, length us, event | category | flops | bytes accessed | tf_op | source)
XLA Modules:
  0.0 62.7 jit_solution(6742938539190520582)
XLA Ops:
  0.6 2.1 %shard_map.78 = f32[64,16,256]{2,1,0:T(8,128)} custom-call(f32[16,1,64,256]{3,2,1,0:T(8,128)} %samples_ref.1), custom_call_target="tpu_custom_call" | custom-call | tf_op jit(solution)/shard_map/pallas_call | solution.py:122
  2.8 0.0 copy-start.3
  2.8 0.0 copy-start.2
  2.8 9.4 %all-to-all-start = ((f32[64,16,256]{2,1,0:T(8,128)}), f32[64,16,256]{2,1,0:T(8,128)S(1)}, u32[]{:S(2)}, u32[]{:S(2)}) async-start(f32[64,16,256]{2,1,0:T(8,128)} %shard_map.78), calls=%async_computation | async-start | bytes 2097152 | tf_op jit(solution)/shard_map/all_to_all | solution.py:281
  12.2 0.0 copy-start.1
  12.2 0.0 copy-done.3
  12.3 0.3 reduce-window.6
  12.5 0.2 slice_reduce_fusion
  12.7 0.2 reduce-window.9
  12.9 0.1 broadcast.13
  13.0 0.1 slice.14
  13.1 0.7 %slice.16 = s32[1,1]{1,0:T(1,128)} slice(s32[1,1024]{1,0:T(1,128)S(1)} %get-tuple-element.25.ends_ref), slice={[0:1], [1023:1024]} | slice | bytes 8 | tf_op jit(solution)/shard_map/slice | solution.py:74
  13.8 0.8 %pad_add_fusion.1.edges = s32[5]{0:T(128)S(1)} fusion(s32[1]{0:T(128)} %bitcast.8, s32[4]{0:T(128)S(1)} %bitcast.31), kind=kLoop, calls=%fused_computation.4 | loop fusion | flops 5 | bytes 40 | tf_op jit(solution)/shard_map/concatenate | solution.py:74
  14.5 0.0 copy-done.2
  14.5 0.0 copy-done.1
  14.5 9.8 %shard_map.77 = (bf16[512,1024]{1,0:T(8,128)(2,1)S(1)}, bf16[512,1024]{1,0:T(8,128)(2,1)S(1)}) custom-call(s32[5]{0:T(128)S(1)} %pad_add_fusion.1.edges, s32[1,1024]{1,0:T(1,128)S(1)} %get-tuple-element.24.starts_ref, s32[1,1024]{1,0:T(1,128)S(1)} %get-tuple-element.25.ends_ref, s32[1,16384]{1,0:T(1,128)S(1)} %bitcast.24, s32[1,16384]{1,0:T(1,128)S(1)} %bitcast.25), custom_call_target="tpu_custom_call" | custom-call | flops 4697620480 | bytes 2097152 | tf_op jit(solution)/shard_map/pallas_call | solution.py:76
  24.3 4.2 %all-to-all-done = f32[64,16,256]{2,1,0:T(8,128)S(1)} async-done(((f32[64,16,256]{2,1,0:T(8,128)}), f32[64,16,256]{2,1,0:T(8,128)S(1)}, u32[]{:S(2)}, u32[]{:S(2)}) %all-to-all-start) | async-done | bytes 1048608 | tf_op jit(solution)/shard_map/all_to_all | solution.py:281
  28.6 0.4 shard_map.79
  29.0 3.4 %collective-permute-start.2 = (f32[128,256]{1,0:T(8,128)S(1)}, f32[128,256]{1,0:T(8,128)S(1)}, u32[]{:S(2)}, u32[]{:S(2)}) collective-permute-start(f32[128,256]{1,0:T(8,128)S(1)} %get-tuple-element.20), channel_id=1, source_target_pairs={{0,1},{1,0},{2,3},{3,2},{4,7},{5,6},{6,5},{7,4},{8,9},{9,8},{10,11... | collective-permute-start | bytes 393224 | tf_op jit(solution)/shard_map/ppermute | solution.py:279
  32.4 0.4 shard_map.81
  32.7 0.1 collective-permute-start
  32.8 0.1 pad_add_fusion.picks
  32.9 1.1 %shard_map.80 = (f32[128,256]{1,0:T(8,128)S(1)}, f32[128,256]{1,0:T(8,128)S(1)}) custom-call(s32[2]{0:T(128)S(1)} %pad_add_fusion.picks, bf16[512,1024]{1,0:T(8,128)(2,1)S(1)} %get-tuple-element.13.high_ref, bf16[512,1024]{1,0:T(8,128)(2,1)S(1)} %get-tuple-element.14.low_ref, bf16[1024,256]{1,0:T(8,128)(2,1)S(1)} %get-tuple-element.15.upper_ref, ...), custom_call_target="tpu_custom_call" | custom-call | flops 402653184 | bytes 3145728 | tf_op jit(solution)/shard_map/pallas_call | solution.py:184
  34.0 5.3 %collective-permute-done.two_ref = f32[128,256]{1,0:T(8,128)S(1)} collective-permute-done((f32[128,256]{1,0:T(8,128)S(1)}, f32[128,256]{1,0:T(8,128)S(1)}, u32[]{:S(2)}, u32[]{:S(2)}) %collective-permute-start) | collective-permute-done | bytes 131104 | tf_op jit(solution)/shard_map/ppermute | solution.py:279
  39.4 0.0 copy-start
  39.4 5.1 %collective-permute-start.1 = (f32[128,256]{1,0:T(8,128)S(1)}, f32[128,256]{1,0:T(8,128)S(1)}, u32[]{:S(2)}, u32[]{:S(2)}) collective-permute-start(f32[128,256]{1,0:T(8,128)S(1)} %shard_map.82.mine_ref), channel_id=1, source_target_pairs={{0,3},{1,2},{2,1},{3,0},{4,5},{5,4},{6,7},{7,6},{8,11},{9,10},{10,... | collective-permute-start | bytes 393224 | tf_op jit(solution)/shard_map/ppermute | solution.py:279
  44.5 0.0 collective-permute-done.2.two_ref
  44.6 0.0 copy-start.4
  44.6 0.1 collective-permute-start.3
  44.7 0.6 copy-done.4
  45.3 0.1 copy.9.state_ref
  45.4 0.1 pad_add_fusion.2.picks
  45.5 2.2 %collective-permute-done.1.other_ref = f32[128,256]{1,0:T(8,128)S(1)} collective-permute-done((f32[128,256]{1,0:T(8,128)S(1)}, f32[128,256]{1,0:T(8,128)S(1)}, u32[]{:S(2)}, u32[]{:S(2)}) %collective-permute-start.1) | collective-permute-done | bytes 131104 | tf_op jit(solution)/shard_map/ppermute | solution.py:279
  47.7 0.0 copy-done
  47.7 0.2 shard_map.83
  47.9 2.9 %collective-permute-start.5 = (f32[128,256]{1,0:T(8,128)S(1)}, f32[128,256]{1,0:T(8,128)S(1)}, u32[]{:S(2)}, u32[]{:S(2)}) collective-permute-start(f32[128,256]{1,0:T(8,128)S(1)} %get-tuple-element.23.refs_0_), channel_id=1, source_target_pairs={{0,1},{1,0},{2,3},{3,2},{4,7},{5,6},{6,5},{7,4},{8,9},{9,8},{10,11... | collective-permute-start | bytes 393224 | tf_op jit(solution)/shard_map/ppermute | solution.py:279
  50.9 1.1 %collective-permute-done.3.other_ref = f32[128,256]{1,0:T(8,128)S(1)} collective-permute-done((f32[128,256]{1,0:T(8,128)S(1)}, f32[128,256]{1,0:T(8,128)S(1)}, u32[]{:S(2)}, u32[]{:S(2)}) %collective-permute-start.3) | collective-permute-done | bytes 131104 | tf_op jit(solution)/shard_map/ppermute | solution.py:279
  51.9 0.2 shard_map.85
  52.1 7.0 %collective-permute-start.4 = (f32[128,256]{1,0:T(8,128)S(1)}, f32[128,256]{1,0:T(8,128)S(1)}, u32[]{:S(2)}, u32[]{:S(2)}) collective-permute-start(f32[128,256]{1,0:T(8,128)S(1)} %get-tuple-element.22.refs_1_), channel_id=1, source_target_pairs={{0,1},{1,0},{2,3},{3,2},{4,7},{5,6},{6,5},{7,4},{8,9},{9,8},{10,11... | collective-permute-start | bytes 393224 | tf_op jit(solution)/shard_map/ppermute | solution.py:279
  59.1 0.7 %select_bitcast_fusion = f32[1,128,256]{2,1,0:T(8,128)} fusion(f32[128,256]{1,0:T(8,128)S(1)} %get-tuple-element.18, f32[128,256]{1,0:T(8,128)S(1)} %get-tuple-element.21, pred[]{:T(512)S(6)} %eq.9), kind=kLoop, calls=%fused_computation | loop fusion | flops 32768 | bytes 393217 | tf_op jit(solution)/shard_map/broadcast_in_dim | solution.py:299
  59.8 0.0 collective-permute-done.5.refs_2_
  59.8 1.3 %shard_map.86.refs_1_ = f32[1,512,256]{2,1,0:T(8,128)} custom-call(s32[3]{0:T(128)S(1)} %pad_add_fusion.2.picks, f32[128,256]{1,0:T(8,128)S(1)} %get-tuple-element.23.refs_0_, f32[128,256]{1,0:T(8,128)S(1)} %get-tuple-element.22.refs_1_, f32[128,256]{1,0:T(8,128)S(1)} %collective-permute-done.5.refs_2_), custom_call_target="tpu_custom_call" | custom-call | tf_op jit(solution)/shard_map/pallas_call | solution.py:248
  61.1 1.0 %collective-permute-done.4.refs_0_ = f32[128,256]{1,0:T(8,128)S(1)} collective-permute-done((f32[128,256]{1,0:T(8,128)S(1)}, f32[128,256]{1,0:T(8,128)S(1)}, u32[]{:S(2)}, u32[]{:S(2)}) %collective-permute-start.4) | collective-permute-done | bytes 131104 | tf_op jit(solution)/shard_map/ppermute | solution.py:279
  62.1 0.7 %shard_map.87 = f32[1,512,256]{2,1,0:T(8,128)} custom-call(s32[1]{0:T(128)} %bitcast.11.picks, f32[128,256]{1,0:T(8,128)S(1)} %collective-permute-done.4.refs_0_, f32[1,512,256]{2,1,0:T(8,128)} %shard_map.86.refs_1_), custom_call_target="tpu_custom_call", output_to_operand_aliasing={{}: (2, {})} | custom-call | tf_op jit(solution)/shard_map/pallas_call | solution.py:248
  (4 shorter events, 0.0 us)
Async XLA Ops:
  2.8 9.5 %copy-start.3 = (s32[1,1,1024]{2,1,0:T(1,128)S(1)}, s32[1,1,1024]{2,1,0:T(1,128)}, u32[]{:S(2)}) copy-start(s32[1,1,1024]{2,1,0:T(1,128)} %param.7) | copy-start | bytes 12292
  2.8 11.7 %copy-start.2 = (s32[1,1,16384]{2,1,0:T(1,128)S(1)}, s32[1,1,16384]{2,1,0:T(1,128)}, u32[]{:S(2)}) copy-start(s32[1,1,16384]{2,1,0:T(1,128)} %param.9) | copy-start | bytes 196612
  2.8 25.8 %all-to-all-start = ((f32[64,16,256]{2,1,0:T(8,128)}), f32[64,16,256]{2,1,0:T(8,128)S(1)}, u32[]{:S(2)}, u32[]{:S(2)}) async-start(f32[64,16,256]{2,1,0:T(8,128)} %shard_map.78), calls=%async_computation | async-start | bytes 2097152 | tf_op jit(solution)/shard_map/all_to_all | solution.py:281
  12.2 2.3 %copy-start.1 = (s32[1,1,16384]{2,1,0:T(1,128)S(1)}, s32[1,1,16384]{2,1,0:T(1,128)}, u32[]{:S(2)}) copy-start(s32[1,1,16384]{2,1,0:T(1,128)} %param.8) | copy-start | bytes 196612
  29.0 15.5 %collective-permute-start.2 = (f32[128,256]{1,0:T(8,128)S(1)}, f32[128,256]{1,0:T(8,128)S(1)}, u32[]{:S(2)}, u32[]{:S(2)}) collective-permute-start(f32[128,256]{1,0:T(8,128)S(1)} %get-tuple-element.20), channel_id=1, source_target_pairs={{0,1},{1,0},{2,3},{3,2},{4,7},{5,6},{6,5},{7,4},{8,9},{9,8},{10,11... | collective-permute-start | bytes 393224 | tf_op jit(solution)/shard_map/ppermute | solution.py:279
  32.7 6.6 %collective-permute-start = (f32[128,256]{1,0:T(8,128)S(1)}, f32[128,256]{1,0:T(8,128)S(1)}, u32[]{:S(2)}, u32[]{:S(2)}) collective-permute-start(f32[128,256]{1,0:T(8,128)S(1)} %shard_map.81), channel_id=1, source_target_pairs={{0,1},{1,0},{2,3},{3,2},{4,7},{5,6},{6,5},{7,4},{8,9},{9,8},{10,11... | collective-permute-start | bytes 393224 | tf_op jit(solution)/shard_map/ppermute | solution.py:279
  39.4 8.3 %copy-start = (f32[1,512,256]{2,1,0:T(8,128)S(1)}, f32[1,512,256]{2,1,0:T(8,128)}, u32[]{:S(2)}) copy-start(f32[1,512,256]{2,1,0:T(8,128)} %param.10) | copy-start | bytes 1572868
  39.4 8.3 %collective-permute-start.1 = (f32[128,256]{1,0:T(8,128)S(1)}, f32[128,256]{1,0:T(8,128)S(1)}, u32[]{:S(2)}, u32[]{:S(2)}) collective-permute-start(f32[128,256]{1,0:T(8,128)S(1)} %shard_map.82.mine_ref), channel_id=1, source_target_pairs={{0,3},{1,2},{2,1},{3,0},{4,5},{5,4},{6,7},{7,6},{8,11},{9,10},{10,... | collective-permute-start | bytes 393224 | tf_op jit(solution)/shard_map/ppermute | solution.py:279
  44.6 0.7 %copy-start.4 = (f32[1,512]{1,0:T(1,128)S(1)}, f32[1,512]{1,0:T(1,128)}, u32[]{:S(2)}) copy-start(f32[1,512]{1,0:T(1,128)} %param.11) | copy-start | bytes 6148
  44.6 7.3 %collective-permute-start.3 = (f32[128,256]{1,0:T(8,128)S(1)}, f32[128,256]{1,0:T(8,128)S(1)}, u32[]{:S(2)}, u32[]{:S(2)}) collective-permute-start(f32[128,256]{1,0:T(8,128)S(1)} %shard_map.84.mine_ref), channel_id=1, source_target_pairs={{0,3},{1,2},{2,1},{3,0},{4,5},{5,4},{6,7},{7,6},{8,11},{9,10},{10,... | collective-permute-start | bytes 393224 | tf_op jit(solution)/shard_map/ppermute | solution.py:279
  47.9 11.9 %collective-permute-start.5 = (f32[128,256]{1,0:T(8,128)S(1)}, f32[128,256]{1,0:T(8,128)S(1)}, u32[]{:S(2)}, u32[]{:S(2)}) collective-permute-start(f32[128,256]{1,0:T(8,128)S(1)} %get-tuple-element.23.refs_0_), channel_id=1, source_target_pairs={{0,1},{1,0},{2,3},{3,2},{4,7},{5,6},{6,5},{7,4},{8,9},{9,8},{10,11... | collective-permute-start | bytes 393224 | tf_op jit(solution)/shard_map/ppermute | solution.py:279
  52.1 9.9 %collective-permute-start.4 = (f32[128,256]{1,0:T(8,128)S(1)}, f32[128,256]{1,0:T(8,128)S(1)}, u32[]{:S(2)}, u32[]{:S(2)}) collective-permute-start(f32[128,256]{1,0:T(8,128)S(1)} %get-tuple-element.22.refs_1_), channel_id=1, source_target_pairs={{0,1},{1,0},{2,3},{3,2},{4,7},{5,6},{6,5},{7,4},{8,9},{9,8},{10,11... | collective-permute-start | bytes 393224 | tf_op jit(solution)/shard_map/ppermute | solution.py:279
